TPU v7x, 32 devices: a whole 2x2x4 slice. The times are simulated.
32 devices in a mesh: rep: 2 (over core), fsdp: 16 (over z, y, x).
Axes of the slice: x: 2, y: 2, z: 4, core: 2. Of those that a mesh axis runs over, the one named last changes fastest.
Arguments:
- attn_out: bfloat16 [49152, 512], P(('rep', 'fsdp')), may hold values from -6 to 6
- cotangent: bfloat16 [49152, 1024], P(('rep', 'fsdp')), may hold values from -6 to 6
- numer: float32 [2, 1024, 512], P('rep', 'fsdp'), may hold values from -6 to 6
- push_weight: float32 [2], P('rep'), may hold values from 0.5 to 2
- moment1: float32 [2, 1024, 512], P('rep', 'fsdp'), may hold values from -0.06 to 0.06
- moment2: float32 [2, 1024, 512], P('rep', 'fsdp'), may hold values from 1e-05 to 0.001
- step_index: int32 [1], replicated, may hold values from 0 to 7
- token_count: int32 [2], P('rep'), may hold values from 12288 to 24576
Outputs:
- mixed_numer: float32 [2, 1024, 512], P('rep', 'fsdp')
- mixed_weight: float32 [2], P('rep')
- new_moment1: float32 [2, 1024, 512], P('rep', 'fsdp')
- new_moment2: float32 [2, 1024, 512], P('rep', 'fsdp')
All inputs are finite; a program needn't handle non-finite values.
Results may differ from a plain program's by a relative error of at most 0.0003.
Values sent between devices are 32-bit elements; how exact they have to be, the bound alone decides.
No kernel may reach another device: no remote copies, remote signals or barrier semaphores. Data moves between devices by JAX's collectives and lax.ppermute only.
A program may use at most 64 MiB of HBM per device.

v0:
```python
import jax
import jax.numpy as jnp
from jax import lax
from jax.sharding import PartitionSpec as P


def local(attn_out, cotangent, numer, push_weight, moment1, moment2, step_index, token_count):
    tok_rows = attn_out.shape[0]
    owned = numer.shape[1]
    count = token_count[0]
    position = lax.axis_index("fsdp") * tok_rows + jnp.arange(tok_rows, dtype=jnp.int32)
    masked = jnp.where((position < count)[:, None], attn_out, jnp.zeros_like(attn_out))
    partial_grad = lax.dot_general(
        cotangent, masked, (((0,), (0,)), ((), ())), preferred_element_type=jnp.float32
    )
    whole_grad = lax.psum(partial_grad, "fsdp")
    total = lax.dynamic_slice_in_dim(whole_grad, lax.axis_index("fsdp") * owned, owned, 0)
    grad = (total / count.astype(jnp.float32))[None]
    step = step_index[0]
    t_value = (step + 1).astype(jnp.float32)
    beta_one = jnp.float32(0.9)
    beta_two = jnp.float32(0.95)
    new_moment1 = beta_one * moment1 + (1.0 - beta_one) * grad
    new_moment2 = beta_two * moment2 + (1.0 - beta_two) * grad * grad
    weight_col = push_weight[:, None, None]
    debiased = numer / weight_col
    first_hat = new_moment1 / (1.0 - jnp.power(beta_one, t_value))
    second_hat = new_moment2 / (1.0 - jnp.power(beta_two, t_value))
    update = first_hat / (jnp.sqrt(second_hat) + 1e-08) + 0.1 * debiased
    stepped = numer - 0.02 * weight_col * update
    bit_count = lax.axis_size("rep").bit_length() - 1
    bit = step % bit_count
    every_numer, every_weight = (
        lax.all_gather(stepped, "rep", axis=0, tiled=True),
        lax.all_gather(push_weight, "rep", axis=0, tiled=True),
    )
    mate = jnp.bitwise_xor(lax.axis_index("rep"), jnp.left_shift(jnp.int32(1), bit))
    mate_numer = lax.dynamic_slice_in_dim(every_numer, mate, 1, 0)
    mate_weight = lax.dynamic_slice_in_dim(every_weight, mate, 1, 0)
    mixed_numer = 0.75 * stepped + 0.25 * mate_numer
    mixed_weight = 0.75 * push_weight + 0.25 * mate_weight
    return (mixed_numer, mixed_weight, new_moment1, new_moment2)


def solution(mesh):
    placed = (
        P(("rep", "fsdp"), None),
        P(("rep", "fsdp"), None),
        P("rep", "fsdp", None),
        P("rep"),
        P("rep", "fsdp", None),
        P("rep", "fsdp", None),
        P(),
        P("rep"),
    )
    return jax.shard_map(
        local,
        mesh=mesh,
        in_specs=placed,
        out_specs=(
            P("rep", "fsdp", None),
            P("rep"),
            P("rep", "fsdp", None),
            P("rep", "fsdp", None),
        ),
        check_vma=False,
    )
```

profile of v0, /device:TPU:0, one launch (start us, length us, event | category | flops | bytes accessed | tf_op | source)
XLA Modules:
  0.0 154.9 jit_solution(6415214981871457468)
XLA Ops:
  7.2 0.0 copy-start
  7.2 0.0 all-reduce.3.cloned.1.call-start
  8.0 1.0 copy-done
  9.1 4.6 %convolution_bitcast_fusion = f32[1024,512]{1,0:T(8,128)} fusion(bf16[1536,1024]{1,0:T(8,128)(2,1)S(1)} %copy-done, bf16[1536,512]{1,0:T(8,128)(2,1)} %param.8, pred[1536]{0:T(1024)(128)(4,1)S(1)} %add_compare_fusion), kind=kOutput, calls=%fused_computation | convolution fusion | flops 1611399168 | bytes 6817280 | tf_op jit(solution)/shard_map/dot_general | solution.py:13
  13.7 0.0 copy-start.4
  13.7 0.0 copy-start.1
  13.7 0.0 copy-start.2
  13.7 0.0 copy-start.3
  13.7 0.0 all-reduce.3.cloned.1.call-update
  14.4 0.0 copy-done.4
  14.5 0.6 dynamic-slice
  15.0 0.8 dynamic-update-slice
  15.8 2.6 %all-reduce = f32[2]{0:T(128)S(1)} all-reduce(f32[2]{0:T(128)S(1)} %dynamic-update-slice), channel_id=1, replica_groups=mesh['rep'=2,'fsdp'=16] {'rep'}, use_global_device_ids=true, to_apply=%add | all-reduce | flops 2 | bytes 16
  19.1 0.6 dynamic_slice.11
  20.3 122.2 %all-reduce.3.cloned.1.call-done = f32[1024,512]{1,0:T(8,128)} async-done(((f32[1024,512]{1,0:T(8,128)}), f32[1024,512]{1,0:T(8,128)}) %all-reduce.3.cloned.1.call-update) | async-done | bytes 2097168 | tf_op jit(solution)/shard_map/psum | solution.py:16
  142.6 0.0 copy-done.1
  142.6 0.0 copy-done.2
  142.6 0.0 copy-done.3
  142.6 1.7 %multiply_subtract_fusion = (f32[1,64,512]{2,1,0:T(8,128)S(1)}, f32[1,64,512]{2,1,0:T(8,128)}, f32[1,64,512]{2,1,0:T(8,128)}) fusion(f32[1,64,512]{2,1,0:T(8,128)S(1)} %copy-done.1, f32[]{:T(128)} %bitcast.17, f32[]{:T(128)} %bitcast.6, f32[]{:T(128)} %bitcast.4, f32[]{:T(128)} %bitcast, f32[]{:T(128)S(6)} %convert_element_type.7, ...), kind=kLoop, calls=%fused_computation.9 | loop fusion | flops 557056 | bytes 917528 | tf_op jit(solution)/shard_map/sub | solution.py:30
  144.3 2.0 %all_gather.6 = f32[2,64,512]{2,1,0:T(8,128)S(1)} all-gather(f32[1,64,512]{2,1,0:T(8,128)S(1)} %get-tuple-element.12), channel_id=1, replica_groups=mesh['rep'=2,'fsdp'=16] {'rep'}, dimensions={0}, use_global_device_ids=true | all-gather | bytes 393216 | tf_op jit(solution)/shard_map/all_gather | solution.py:34
  146.3 0.7 multiply_add_fusion
  (2 shorter events, 0.0 us)
Async XLA Ops:
  7.2 1.9 %copy-start = (bf16[1536,1024]{1,0:T(8,128)(2,1)S(1)}, bf16[1536,1024]{1,0:T(8,128)(2,1)}, u32[]{:S(2)}) copy-start(bf16[1536,1024]{1,0:T(8,128)(2,1)} %param.9) | copy-start | bytes 9437188
  7.2 135.4 %all-reduce.3.cloned.1.call-start = ((), (), s32[]{:S(2)}) async-start(), calls=%async_computation | async-start | bytes 4194304 | tf_op jit(solution)/shard_map/psum | solution.py:16
  13.7 0.7 copy-start.4
  13.7 128.9 %copy-start.1 = (f32[1,64,512]{2,1,0:T(8,128)S(1)}, f32[1,64,512]{2,1,0:T(8,128)}, u32[]{:S(2)}) copy-start(f32[1,64,512]{2,1,0:T(8,128)} %param.10) | copy-start | bytes 393220
  13.7 128.9 %copy-start.2 = (f32[1,64,512]{2,1,0:T(8,128)S(1)}, f32[1,64,512]{2,1,0:T(8,128)}, u32[]{:S(2)}) copy-start(f32[1,64,512]{2,1,0:T(8,128)} %param.13) | copy-start | bytes 393220
  13.7 128.9 %copy-start.3 = (f32[1,64,512]{2,1,0:T(8,128)S(1)}, f32[1,64,512]{2,1,0:T(8,128)}, u32[]{:S(2)}) copy-start(f32[1,64,512]{2,1,0:T(8,128)} %param.12) | copy-start | bytes 393220
Sparse Core Ops, SparseCore 0:
  13.9 128.6 all-reduce.2
where the time goes:
time: 155 us
  waiting for transfers between devices  122 us (79%)
  between operations  18.1 us (12%)
  matrix products  4.62 us (3%)
  blocking collectives  4.54 us (3%)
  local copies, waits for them, and re-layouts  2.99 us (2%)
  other arithmetic  2.39 us (2%)
    psum x1, waiting for transfers between devices, local(): whole_grad = lax.psum(partial_grad, 'fsdp')  122 us
    dot_general x1, matrix products, local(): lax.dot_general(cotangent, masked, (((0,), (0,)), ((), ())), preferred_el...  4.62 us
  transfers between devices with their start and end apart: 1, of which 1 were waited for; matrix products, arithmetic and copies ran while one was open for 1% of the time, Pallas kernels for 0%

commit v1 on v0

v1 whole, which is shorter than its diff:
```python
import functools
import jax
import jax.numpy as jnp
from jax import lax
from jax.experimental import pallas as pl
from jax.experimental.pallas import tpu as pltpu
from jax.sharding import PartitionSpec as P

ORDERS = (
    ((4, 2, 1, 8), (2, 1, 8, 4)),
    ((1, 8, 4, 2), (1, 4, 2, 8)),
)
SHARE = 0.625


def orders_of(size):
    if size == 16:
        return ORDERS
    bits = tuple(1 << k for k in range(size.bit_length() - 1))
    turned = bits[1:] + bits[:1]
    return ((bits, turned), (bits[::-1], turned[::-1]))


def rows_of(owned):
    first = min(max(8, 8 * round(SHARE * owned / 8)), owned - 8)
    return (first, owned - first)


def place(relative, order):
    top = len(order) - 1
    spot = 0
    for k, bit in enumerate(order):
        low = bit.bit_length() - 1
        spot = spot | (((relative >> low) & 1) << (top - k))
    return spot


def product_kernel(orders, rows, owned, tok_rows, group, info, attn, cot, *rest):
    outs, masked = rest[:4], rest[4]
    me, core, count = info[0], info[1], info[2]
    step = pl.program_id(0)

    @pl.when(step == 0)
    def _():
        position = me * tok_rows + lax.broadcasted_iota(jnp.int32, attn.shape, 0)
        live = position < count
        masked[...] = jnp.where(live, attn[...].astype(jnp.float32), 0.0).astype(masked.dtype)

    result = lax.dot_general(
        cot[...], masked[...], (((0,), (0,)), ((), ())), preferred_element_type=jnp.float32
    )
    half = 1 << (len(orders[0][0]) - 1)
    for s in range(group):
        relative = me ^ (step * group + s)
        base = s * owned
        for c, (even, odd) in enumerate(orders):
            spot = jnp.where(core == 0, place(relative, even), place(relative, odd))
            piece = result[base:base + rows[c]]
            base += rows[c]

            @pl.when(spot >= half)
            def _():
                outs[2 * c][spot - half] = piece

            @pl.when(spot < half)
            def _():
                outs[2 * c + 1][spot] = piece


def product(attn_out, cotangent, me, core, count, orders, rows):
    tok_rows, width = attn_out.shape
    owned = sum(rows)
    devices = cotangent.shape[1] // owned
    group = max(1, 256 // owned)
    info = jnp.stack([me, core, count])
    half = devices // 2
    return pl.pallas_call(
        functools.partial(product_kernel, orders, rows, owned, tok_rows, group),
        out_shape=[
            jax.ShapeDtypeStruct((half, r, width), jnp.float32) for r in rows for _ in range(2)
        ],
        grid_spec=pltpu.PrefetchScalarGridSpec(
            num_scalar_prefetch=1,
            grid=(devices // group,),
            in_specs=[
                pl.BlockSpec((tok_rows, width), lambda i, s: (0, 0)),
                pl.BlockSpec((tok_rows, group * owned), lambda i, s: (0, i)),
            ],
            out_specs=[
                pl.BlockSpec((half, r, width), lambda i, s: (0, 0, 0))
                for r in rows for _ in range(2)
            ],
            scratch_shapes=[pltpu.VMEM((tok_rows, width), jnp.bfloat16)],
        ),
        compiler_params=pltpu.CompilerParams(vmem_limit_bytes=40 * 1024 * 1024),
        cost_estimate=pl.CostEstimate(
            flops=2 * tok_rows * width * cotangent.shape[1],
            bytes_accessed=2 * tok_rows * (width + cotangent.shape[1]) + 4 * width * cotangent.shape[1],
            transcendentals=0,
        ),
    )(info, attn_out, cotangent)


def swap(value, pair, reps, devices):
    pairs = [
        (r * devices + f, r * devices + (f ^ pair[r % 2]))
        for r in range(reps) for f in range(devices)
    ]
    return lax.ppermute(value, ("rep", "fsdp"), pairs)


def local(attn_out, cotangent, numer, push_weight, moment1, moment2, step_index, token_count):
    owned = numer.shape[1]
    reps, devices = lax.axis_size("rep"), lax.axis_size("fsdp")
    count = token_count[0]
    me, core = lax.axis_index("fsdp"), lax.axis_index("rep") % 2
    orders, rows = orders_of(devices), rows_of(owned)
    blocks = product(attn_out, cotangent, me, core, count, orders, rows)

    send, keep = list(blocks[0::2]), list(blocks[1::2])
    stages = devices.bit_length() - 1
    for k in range(stages):
        got = [swap(send[c], (orders[c][0][k], orders[c][1][k]), reps, devices) for c in range(2)]
        for c in range(2):
            if k < stages - 1:
                half = keep[c].shape[0] // 2
                send[c] = keep[c][half:] + got[c][half:]
                keep[c] = keep[c][:half] + got[c][:half]
            else:
                keep[c] = keep[c] + got[c]
    total = jnp.concatenate([keep[0], keep[1]], axis=1)
    grad = total / count.astype(jnp.float32)
    step = step_index[0]
    t_value = (step + 1).astype(jnp.float32)
    beta_one = jnp.float32(0.9)
    beta_two = jnp.float32(0.95)
    new_moment1 = beta_one * moment1 + (1.0 - beta_one) * grad
    new_moment2 = beta_two * moment2 + (1.0 - beta_two) * grad * grad
    weight_col = push_weight[:, None, None]
    debiased = numer / weight_col
    first_hat = new_moment1 / (1.0 - jnp.power(beta_one, t_value))
    second_hat = new_moment2 / (1.0 - jnp.power(beta_two, t_value))
    update = first_hat / (jnp.sqrt(second_hat) + 1e-08) + 0.1 * debiased
    stepped = numer - 0.02 * weight_col * update

    def exchange(bit, values):
        pairs = [(r, r ^ (1 << bit)) for r in range(reps)]
        return tuple(lax.ppermute(v, "rep", pairs) for v in values)

    bit_count = reps.bit_length() - 1
    if bit_count == 1:
        (mate_weight,) = exchange(0, (push_weight,))
        (mate_numer,) = exchange(0, (stepped,))
    else:
        mate_weight, mate_numer = lax.switch(
            step % bit_count,
            [functools.partial(exchange, b) for b in range(bit_count)],
            (push_weight, stepped),
        )
    mixed_numer = 0.75 * stepped + 0.25 * mate_numer
    mixed_weight = 0.75 * push_weight + 0.25 * mate_weight
    return (mixed_numer, mixed_weight, new_moment1, new_moment2)


def solution(mesh):
    placed = (
        P(("rep", "fsdp"), None),
        P(("rep", "fsdp"), None),
        P("rep", "fsdp", None),
        P("rep"),
        P("rep", "fsdp", None),
        P("rep", "fsdp", None),
        P(),
        P("rep"),
    )
    return jax.shard_map(
        local,
        mesh=mesh,
        in_specs=placed,
        out_specs=(
            P("rep", "fsdp", None),
            P("rep"),
            P("rep", "fsdp", None),
            P("rep", "fsdp", None),
        ),
        check_vma=False,
    )
```

time: 155 us -> 49.5 us (0.32)
  waiting for transfers between devices: 122 us -> 22.4 us
  between operations: 18.1 us -> 4.47 us
  starting transfers between devices: 0.04 us -> 13 us
  matrix products: 4.62 us -> 0 us
  blocking collectives: 4.54 us -> 0 us
  Pallas kernels: 0 us -> 4.27 us
    psum x1 -> x0, waiting for transfers between devices: 122 us -> none  [local(): whole_grad = lax.psum(partial_grad, 'fsdp')]
    ppermute x0 -> x10, waiting for transfers between devices: none -> 22.4 us  [the longest x8 21.3 us: swap(): return lax.ppermute(value, ('rep', 'fsdp'), pairs)]
    ppermute x0 -> x10, starting transfers between devices: none -> 13 us  [the longest x8 12.5 us: swap(): return lax.ppermute(value, ('rep', 'fsdp'), pairs)]
    dot_general x1 -> x0, matrix products: 4.62 us -> none  [local(): lax.dot_general(cotangent, masked, (((0,), (0,)), ((), ())), preferred_el...]
    pallas_call x0 -> x1, Pallas kernels: none -> 4.27 us  [product(): pl.pallas_call(functools.partial(product_kernel, orders, rows, owned, tok...]
    unnamed x1 -> x0, blocking collectives: 2.56 us -> none
    all_gather x1 -> x0, blocking collectives: 1.98 us -> none  [local(): lax.all_gather(stepped, 'rep', axis=0, tiled=True)]
    unnamed x13 -> x10, local copies, waits for them, and re-layouts: 2.4 us -> 3.32 us
  transfers between devices with their start and end apart: 1 -> 10, of which waited for: 1 -> 8; matrix products, arithmetic and copies ran while one was open for 1% -> 1% of each run, Pallas kernels for 0% -> 0%
where the time goes in v1:
time: 49.5 us; the launch traced here: 49.3 us
  waiting for transfers between devices  22.4 us (45%)
  starting transfers between devices  13 us (26%)
  between operations  4.47 us (9%)
  Pallas kernels  4.27 us (9%)
  local copies, waits for them, and re-layouts  3.32 us (7%)
  other arithmetic  1.86 us (4%)
    ppermute x8, waiting for transfers between devices, swap(): return lax.ppermute(value, ('rep', 'fsdp'), pairs)  21.3 us
    ppermute x8, starting transfers between devices, swap(): return lax.ppermute(value, ('rep', 'fsdp'), pairs)  12.5 us
    pallas_call x1, Pallas kernels, product(): pl.pallas_call(functools.partial(product_kernel, orders, rows, owned, tok...  4.27 us
    unnamed x10, local copies, waits for them, and re-layouts  3.32 us
    ppermute x2, waiting for transfers between devices, exchange(): return tuple((lax.ppermute(v, 'rep', pairs) for v in values))  1.09 us
  transfers between devices with their start and end apart: 10, of which 8 were waited for; matrix products, arithmetic and copies ran while one was open for 1% of the time, Pallas kernels for 0%

profile of v1, /device:TPU:0, one launch (start us, length us, event | category | flops | bytes accessed | tf_op | source)
XLA Modules:
  0.0 49.3 jit_solution(3437399440721412919)
XLA Ops:
  1.3 0.1 pad_add_fusion.info
  1.4 0.0 copy-start
  1.4 1.9 %copy-done = bf16[1536,1024]{1,0:T(8,128)(2,1)S(1)} copy-done((bf16[1536,1024]{1,0:T(8,128)(2,1)S(1)}, bf16[1536,1024]{1,0:T(8,128)(2,1)}, u32[]{:S(2)}) %copy-start) | copy-done | bytes 3145752
  3.3 0.0 copy-start.1
  3.3 1.4 %copy-done.1 = bf16[1536,512]{1,0:T(8,128)(2,1)S(1)} copy-done((bf16[1536,512]{1,0:T(8,128)(2,1)S(1)}, bf16[1536,512]{1,0:T(8,128)(2,1)}, u32[]{:S(2)}) %copy-start.1) | copy-done | bytes 1572888
  4.7 4.3 %shard_map.111 = (f32[8,40,512]{2,1,0:T(8,128)S(1)}, f32[8,40,512]{2,1,0:T(8,128)S(1)}, f32[8,24,512]{2,1,0:T(8,128)S(1)}, f32[8,24,512]{2,1,0:T(8,128)S(1)}) custom-call(s32[3]{0:T(128)S(1)} %pad_add_fusion.info, bf16[1536,512]{1,0:T(8,128)(2,1)S(1)} %copy-done.1, bf16[1536,1024]{1,0:T(8,128)(2,1)S(1)} %copy-done), custom_call_target="tpu_custom_call" | custom-call | flops 1610612736 | bytes 6815744 | tf_op jit(solution)/shard_map/pallas_call | solution.py:77
  8.9 0.0 copy-start.2
  8.9 0.0 copy-start.3
  9.0 0.0 copy-start.4
  9.0 3.1 %collective-permute-start = (f32[8,40,512]{2,1,0:T(8,128)S(1)}, f32[8,40,512]{2,1,0:T(8,128)S(1)}, u32[]{:S(2)}, u32[]{:S(2)}) collective-permute-start(f32[8,40,512]{2,1,0:T(8,128)S(1)} %get-tuple-element.9), channel_id=1, source_target_pairs={{0,4},{1,5},{2,6},{3,7},{4,0},{5,1},{6,2},{7,3},{8,12},{9,13},{10,... | collective-permute-start | bytes 1966088 | tf_op jit(solution)/shard_map/ppermute | solution.py:109
  12.1 1.5 %collective-permute-start.4 = (f32[8,24,512]{2,1,0:T(8,128)S(1)}, f32[8,24,512]{2,1,0:T(8,128)S(1)}, u32[]{:S(2)}, u32[]{:S(2)}) collective-permute-start(f32[8,24,512]{2,1,0:T(8,128)S(1)} %get-tuple-element.11), channel_id=1, source_target_pairs={{0,1},{1,0},{2,3},{3,2},{4,5},{5,4},{6,7},{7,6},{8,9},{9,8},{10,11... | collective-permute-start | bytes 1179656 | tf_op jit(solution)/shard_map/ppermute | solution.py:109
  13.6 9.0 %collective-permute-done.4 = f32[8,24,512]{2,1,0:T(8,128)S(1)} collective-permute-done((f32[8,24,512]{2,1,0:T(8,128)S(1)}, f32[8,24,512]{2,1,0:T(8,128)S(1)}, u32[]{:S(2)}, u32[]{:S(2)}) %collective-permute-start.4) | collective-permute-done | bytes 393248 | tf_op jit(solution)/shard_map/ppermute | solution.py:109
  22.6 0.1 slice_add_fusion.3
  22.6 2.7 %collective-permute-start.5 = (f32[4,24,512]{2,1,0:T(8,128)S(1)}, f32[4,24,512]{2,1,0:T(8,128)S(1)}, u32[]{:S(2)}, u32[]{:S(2)}) collective-permute-start(f32[4,24,512]{2,1,0:T(8,128)S(1)} %get-tuple-element.18), channel_id=1, source_target_pairs={{0,8},{1,9},{2,10},{3,11},{4,12},{5,13},{6,14},{7,15},{8,0},{9,1},... | collective-permute-start | bytes 589832 | tf_op jit(solution)/shard_map/ppermute | solution.py:109
  25.3 0.0 collective-permute-done
  25.3 0.1 slice_add_fusion.1
  25.4 0.6 %collective-permute-start.1 = (f32[4,40,512]{2,1,0:T(8,128)S(1)}, f32[4,40,512]{2,1,0:T(8,128)S(1)}, u32[]{:S(2)}, u32[]{:S(2)}) collective-permute-start(f32[4,40,512]{2,1,0:T(8,128)S(1)} %get-tuple-element.16), channel_id=1, source_target_pairs={{0,2},{1,3},{2,0},{3,1},{4,6},{5,7},{6,4},{7,5},{8,10},{9,11},{10,... | collective-permute-start | bytes 983048 | tf_op jit(solution)/shard_map/ppermute | solution.py:109
  27.4 4.0 %collective-permute-done.5 = f32[4,24,512]{2,1,0:T(8,128)S(1)} collective-permute-done((f32[4,24,512]{2,1,0:T(8,128)S(1)}, f32[4,24,512]{2,1,0:T(8,128)S(1)}, u32[]{:S(2)}, u32[]{:S(2)}) %collective-permute-start.5) | collective-permute-done | bytes 196640 | tf_op jit(solution)/shard_map/ppermute | solution.py:109
  31.4 0.8 %collective-permute-start.6 = (f32[2,24,512]{2,1,0:T(8,128)S(1)}, f32[2,24,512]{2,1,0:T(8,128)S(1)}, u32[]{:S(2)}, u32[]{:S(2)}) collective-permute-start(f32[2,24,512]{2,1,0:T(8,128)S(1)} %get-tuple-element.22), channel_id=1, source_target_pairs={{0,4},{1,5},{2,6},{3,7},{4,0},{5,1},{6,2},{7,3},{8,12},{9,13},{10,... | collective-permute-start | bytes 294920 | tf_op jit(solution)/shard_map/ppermute | solution.py:109
  32.2 1.4 %collective-permute-done.1 = f32[4,40,512]{2,1,0:T(8,128)S(1)} collective-permute-done((f32[4,40,512]{2,1,0:T(8,128)S(1)}, f32[4,40,512]{2,1,0:T(8,128)S(1)}, u32[]{:S(2)}, u32[]{:S(2)}) %collective-permute-start.1) | collective-permute-done | bytes 327712 | tf_op jit(solution)/shard_map/ppermute | solution.py:109
  33.7 1.6 %collective-permute-start.2 = (f32[2,40,512]{2,1,0:T(8,128)S(1)}, f32[2,40,512]{2,1,0:T(8,128)S(1)}, u32[]{:S(2)}, u32[]{:S(2)}) collective-permute-start(f32[2,40,512]{2,1,0:T(8,128)S(1)} %get-tuple-element.20), channel_id=1, source_target_pairs={{0,1},{1,0},{2,3},{3,2},{4,5},{5,4},{6,7},{7,6},{8,9},{9,8},{10,11... | collective-permute-start | bytes 491528 | tf_op jit(solution)/shard_map/ppermute | solution.py:109
  35.2 2.8 %collective-permute-done.6 = f32[2,24,512]{2,1,0:T(8,128)S(1)} collective-permute-done((f32[2,24,512]{2,1,0:T(8,128)S(1)}, f32[2,24,512]{2,1,0:T(8,128)S(1)}, u32[]{:S(2)}, u32[]{:S(2)}) %collective-permute-start.6) | collective-permute-done | bytes 98336 | tf_op jit(solution)/shard_map/ppermute | solution.py:109
  38.0 0.2 collective-permute-start.7
  38.2 0.8 %collective-permute-done.2 = f32[2,40,512]{2,1,0:T(8,128)S(1)} collective-permute-done((f32[2,40,512]{2,1,0:T(8,128)S(1)}, f32[2,40,512]{2,1,0:T(8,128)S(1)}, u32[]{:S(2)}, u32[]{:S(2)}) %collective-permute-start.2) | collective-permute-done | bytes 163872 | tf_op jit(solution)/shard_map/ppermute | solution.py:109
  39.1 2.1 %collective-permute-start.3 = (f32[1,40,512]{2,1,0:T(8,128)S(1)}, f32[1,40,512]{2,1,0:T(8,128)S(1)}, u32[]{:S(2)}, u32[]{:S(2)}) collective-permute-start(f32[1,40,512]{2,1,0:T(8,128)S(1)} %slice_add_fusion.8), channel_id=1, source_target_pairs={{0,8},{1,9},{2,10},{3,11},{4,12},{5,13},{6,14},{7,15},{8,0},{9,1},... | collective-permute-start | bytes 245768 | tf_op jit(solution)/shard_map/ppermute | solution.py:109
  41.1 1.0 %collective-permute-done.7 = f32[1,24,512]{2,1,0:T(8,128)S(1)} collective-permute-done((f32[1,24,512]{2,1,0:T(8,128)S(1)}, f32[1,24,512]{2,1,0:T(8,128)S(1)}, u32[]{:S(2)}, u32[]{:S(2)}) %collective-permute-start.7) | collective-permute-done | bytes 49184 | tf_op jit(solution)/shard_map/ppermute | solution.py:109
  42.2 2.3 %collective-permute-done.3 = f32[1,40,512]{2,1,0:T(8,128)S(1)} collective-permute-done((f32[1,40,512]{2,1,0:T(8,128)S(1)}, f32[1,40,512]{2,1,0:T(8,128)S(1)}, u32[]{:S(2)}, u32[]{:S(2)}) %collective-permute-start.3) | collective-permute-done | bytes 81952 | tf_op jit(solution)/shard_map/ppermute | solution.py:109
  44.5 0.0 copy-done.2
  44.5 0.0 copy-done.3
  44.5 0.0 copy-done.4
  44.5 0.8 %multiply_subtract_fusion = (f32[1,64,512]{2,1,0:T(8,128)S(1)}, f32[1,64,512]{2,1,0:T(8,128)}, f32[1,64,512]{2,1,0:T(8,128)}) fusion(f32[1,64,512]{2,1,0:T(8,128)S(1)} %copy-done.2, f32[]{:T(128)} %bitcast.7, f32[]{:T(128)} %bitcast.5, f32[]{:T(128)} %bitcast.4, f32[]{:T(128)} %bitcast, f32[]{:T(128)} %bitcast.3, f32[1,24,512]{2,1,0:T(8,128)S(1)} %fusion.2, ...), kind=kLoop, calls=%fused_computation.10 | loop fusion | flops 589824 | bytes 917524 | tf_op jit(solution)/shard_map/sub | solution.py:144
  45.3 0.0 collective-permute-start.8
  45.3 0.5 %collective-permute-start.9 = (f32[1]{0:T(128)}, f32[1]{0:T(128)}, u32[]{:S(2)}, u32[]{:S(2)}) collective-permute-start(f32[1]{0:T(128)} %param.11), channel_id=1, source_target_pairs={{0,16},{16,0},{1,17},{17,1},{2,18},{18,2},{3,19},{19,3},{4,20},{20... | collective-permute-start | bytes 20 | tf_op jit(solution)/shard_map/ppermute | solution.py:148
  45.8 1.1 %collective-permute-done.9 = f32[1]{0:T(128)} collective-permute-done((f32[1]{0:T(128)}, f32[1]{0:T(128)}, u32[]{:S(2)}, u32[]{:S(2)}) %collective-permute-start.9) | collective-permute-done | bytes 36 | tf_op jit(solution)/shard_map/ppermute | solution.py:148
  47.5 0.0 collective-permute-done.8
  47.5 0.7 %multiply_add_fusion = f32[1,64,512]{2,1,0:T(8,128)} fusion(f32[1,64,512]{2,1,0:T(8,128)S(1)} %collective-permute-done.8, f32[1,64,512]{2,1,0:T(8,128)S(1)} %get-tuple-element.12), kind=kLoop, calls=%fused_computation.9 | loop fusion | flops 98304 | bytes 393216 | tf_op jit(solution)/shard_map/add | solution.py:160
  (6 shorter events, 0.1 us)
Async XLA Ops:
  1.4 1.9 %copy-start = (bf16[1536,1024]{1,0:T(8,128)(2,1)S(1)}, bf16[1536,1024]{1,0:T(8,128)(2,1)}, u32[]{:S(2)}) copy-start(bf16[1536,1024]{1,0:T(8,128)(2,1)} %cot.1) | copy-start | bytes 9437188
  3.3 1.4 %copy-start.1 = (bf16[1536,512]{1,0:T(8,128)(2,1)S(1)}, bf16[1536,512]{1,0:T(8,128)(2,1)}, u32[]{:S(2)}) copy-start(bf16[1536,512]{1,0:T(8,128)(2,1)} %attn.1) | copy-start | bytes 4718596
  8.9 35.6 %copy-start.2 = (f32[1,64,512]{2,1,0:T(8,128)S(1)}, f32[1,64,512]{2,1,0:T(8,128)}, u32[]{:S(2)}) copy-start(f32[1,64,512]{2,1,0:T(8,128)} %param.10) | copy-start | bytes 393220
  8.9 35.5 %copy-start.3 = (f32[1,64,512]{2,1,0:T(8,128)S(1)}, f32[1,64,512]{2,1,0:T(8,128)}, u32[]{:S(2)}) copy-start(f32[1,64,512]{2,1,0:T(8,128)} %param.13) | copy-start | bytes 393220
  9.0 35.5 %copy-start.4 = (f32[1,64,512]{2,1,0:T(8,128)S(1)}, f32[1,64,512]{2,1,0:T(8,128)}, u32[]{:S(2)}) copy-start(f32[1,64,512]{2,1,0:T(8,128)} %param.12) | copy-start | bytes 393220
  9.0 16.3 %collective-permute-start = (f32[8,40,512]{2,1,0:T(8,128)S(1)}, f32[8,40,512]{2,1,0:T(8,128)S(1)}, u32[]{:S(2)}, u32[]{:S(2)}) collective-permute-start(f32[8,40,512]{2,1,0:T(8,128)S(1)} %get-tuple-element.9), channel_id=1, source_target_pairs={{0,4},{1,5},{2,6},{3,7},{4,0},{5,1},{6,2},{7,3},{8,12},{9,13},{10,... | collective-permute-start | bytes 1966088 | tf_op jit(solution)/shard_map/ppermute | solution.py:109
  12.1 10.5 %collective-permute-start.4 = (f32[8,24,512]{2,1,0:T(8,128)S(1)}, f32[8,24,512]{2,1,0:T(8,128)S(1)}, u32[]{:S(2)}, u32[]{:S(2)}) collective-permute-start(f32[8,24,512]{2,1,0:T(8,128)S(1)} %get-tuple-element.11), channel_id=1, source_target_pairs={{0,1},{1,0},{2,3},{3,2},{4,5},{5,4},{6,7},{7,6},{8,9},{9,8},{10,11... | collective-permute-start | bytes 1179656 | tf_op jit(solution)/shard_map/ppermute | solution.py:109
  22.6 8.8 %collective-permute-start.5 = (f32[4,24,512]{2,1,0:T(8,128)S(1)}, f32[4,24,512]{2,1,0:T(8,128)S(1)}, u32[]{:S(2)}, u32[]{:S(2)}) collective-permute-start(f32[4,24,512]{2,1,0:T(8,128)S(1)} %get-tuple-element.18), channel_id=1, source_target_pairs={{0,8},{1,9},{2,10},{3,11},{4,12},{5,13},{6,14},{7,15},{8,0},{9,1},... | collective-permute-start | bytes 589832 | tf_op jit(solution)/shard_map/ppermute | solution.py:109
  25.4 8.2 %collective-permute-start.1 = (f32[4,40,512]{2,1,0:T(8,128)S(1)}, f32[4,40,512]{2,1,0:T(8,128)S(1)}, u32[]{:S(2)}, u32[]{:S(2)}) collective-permute-start(f32[4,40,512]{2,1,0:T(8,128)S(1)} %get-tuple-element.16), channel_id=1, source_target_pairs={{0,2},{1,3},{2,0},{3,1},{4,6},{5,7},{6,4},{7,5},{8,10},{9,11},{10,... | collective-permute-start | bytes 983048 | tf_op jit(solution)/shard_map/ppermute | solution.py:109
  31.4 6.6 %collective-permute-start.6 = (f32[2,24,512]{2,1,0:T(8,128)S(1)}, f32[2,24,512]{2,1,0:T(8,128)S(1)}, u32[]{:S(2)}, u32[]{:S(2)}) collective-permute-start(f32[2,24,512]{2,1,0:T(8,128)S(1)} %get-tuple-element.22), channel_id=1, source_target_pairs={{0,4},{1,5},{2,6},{3,7},{4,0},{5,1},{6,2},{7,3},{8,12},{9,13},{10,... | collective-permute-start | bytes 294920 | tf_op jit(solution)/shard_map/ppermute | solution.py:109
  33.7 5.4 %collective-permute-start.2 = (f32[2,40,512]{2,1,0:T(8,128)S(1)}, f32[2,40,512]{2,1,0:T(8,128)S(1)}, u32[]{:S(2)}, u32[]{:S(2)}) collective-permute-start(f32[2,40,512]{2,1,0:T(8,128)S(1)} %get-tuple-element.20), channel_id=1, source_target_pairs={{0,1},{1,0},{2,3},{3,2},{4,5},{5,4},{6,7},{7,6},{8,9},{9,8},{10,11... | collective-permute-start | bytes 491528 | tf_op jit(solution)/shard_map/ppermute | solution.py:109
  38.0 4.2 %collective-permute-start.7 = (f32[1,24,512]{2,1,0:T(8,128)S(1)}, f32[1,24,512]{2,1,0:T(8,128)S(1)}, u32[]{:S(2)}, u32[]{:S(2)}) collective-permute-start(f32[1,24,512]{2,1,0:T(8,128)S(1)} %slice_add_fusion.10), channel_id=1, source_target_pairs={{0,2},{1,3},{2,0},{3,1},{4,6},{5,7},{6,4},{7,5},{8,10},{9,11},{10,... | collective-permute-start | bytes 147464 | tf_op jit(solution)/shard_map/ppermute | solution.py:109
  39.1 5.4 %collective-permute-start.3 = (f32[1,40,512]{2,1,0:T(8,128)S(1)}, f32[1,40,512]{2,1,0:T(8,128)S(1)}, u32[]{:S(2)}, u32[]{:S(2)}) collective-permute-start(f32[1,40,512]{2,1,0:T(8,128)S(1)} %slice_add_fusion.8), channel_id=1, source_target_pairs={{0,8},{1,9},{2,10},{3,11},{4,12},{5,13},{6,14},{7,15},{8,0},{9,1},... | collective-permute-start | bytes 245768 | tf_op jit(solution)/shard_map/ppermute | solution.py:109
  45.3 2.2 %collective-permute-start.8 = (f32[1,64,512]{2,1,0:T(8,128)S(1)}, f32[1,64,512]{2,1,0:T(8,128)S(1)}, u32[]{:S(2)}, u32[]{:S(2)}) collective-permute-start(f32[1,64,512]{2,1,0:T(8,128)S(1)} %get-tuple-element.12), channel_id=1, source_target_pairs={{0,16},{16,0},{1,17},{17,1},{2,18},{18,2},{3,19},{19,3},{4,20},{20... | collective-permute-start | bytes 393224 | tf_op jit(solution)/shard_map/ppermute | solution.py:148
  45.3 1.6 %collective-permute-start.9 = (f32[1]{0:T(128)}, f32[1]{0:T(128)}, u32[]{:S(2)}, u32[]{:S(2)}) collective-permute-start(f32[1]{0:T(128)} %param.11), channel_id=1, source_target_pairs={{0,16},{16,0},{1,17},{17,1},{2,18},{18,2},{3,19},{19,3},{4,20},{20... | collective-permute-start | bytes 20 | tf_op jit(solution)/shard_map/ppermute | solution.py:148

commit v2 on v0

v2 whole, which is shorter than its diff:
```python
import functools
import jax
import jax.numpy as jnp
from jax import lax
from jax.experimental import pallas as pl
from jax.experimental.pallas import tpu as pltpu
from jax.sharding import PartitionSpec as P

ORDERS = (
    ((4, 1, 8, 2), (1, 2, 8, 4)),
    ((4, 2, 1, 8), (2, 1, 4, 8)),
)
SHARE = 0.5


def orders_of(size):
    if size == 16:
        return ORDERS
    bits = tuple(1 << k for k in range(size.bit_length() - 1))
    turned = bits[1:] + bits[:1]
    return ((bits, turned), (bits[::-1], turned[::-1]))


def rows_of(owned):
    first = min(max(8, 8 * round(SHARE * owned / 8)), owned - 8)
    return (first, owned - first)


def place(relative, order):
    top = len(order) - 1
    spot = 0
    for k, bit in enumerate(order):
        low = bit.bit_length() - 1
        spot = spot | (((relative >> low) & 1) << (top - k))
    return spot


def product_kernel(orders, rows, owned, slabs, columns, count, attn, cot, *rest):
    outs = rest[:len(orders)]
    attn_v, cot_v, total, attn_sems, cot_sems = rest[len(orders):]
    tok_rows, width = attn.shape
    me, core = lax.axis_index("fsdp"), lax.axis_index("rep") % 2
    depth = tok_rows // slabs
    spans = [pl.ds(k * depth, depth) for k in range(slabs)]
    attn_in = [
        pltpu.make_async_copy(attn.at[span], attn_v.at[span], attn_sems.at[k])
        for k, span in enumerate(spans)
    ]
    cot_in = [
        pltpu.make_async_copy(cot.at[span], cot_v.at[span], cot_sems.at[k])
        for k, span in enumerate(spans)
    ]
    for k in range(slabs):
        attn_in[k].start()
        cot_in[k].start()
    live = count[0] - me * tok_rows

    def put(first, result):
        for s in range(columns // owned):
            relative = me ^ (first // owned + s)
            base = s * owned
            for c, (even, odd) in enumerate(orders):
                spot = jnp.where(core == 0, place(relative, even), place(relative, odd))
                outs[c][spot] = result[base:base + rows[c]]
                base += rows[c]

    for k, span in enumerate(spans):
        attn_in[k].wait()

        @pl.when(live < (k + 1) * depth)
        def _():
            position = k * depth + lax.broadcasted_iota(jnp.int32, (depth, width), 0)
            kept = jnp.where(position < live, attn_v[span].astype(jnp.float32), 0.0)
            attn_v[span] = kept.astype(attn_v.dtype)

        cot_in[k].wait()
        for first in range(0, cot.shape[1], columns):
            part = pl.ds(first, columns)
            term = lax.dot_general(
                cot_v[span, part], attn_v[span], (((0,), (0,)), ((), ())),
                preferred_element_type=jnp.float32,
            )
            if k > 0:
                term = total[part] + term
            if k < slabs - 1:
                total[part] = term
            else:
                put(first, term)


def product(attn_out, cotangent, token_count, orders, rows):
    tok_rows, width = attn_out.shape
    owned = sum(rows)
    features = cotangent.shape[1]
    slabs = 6 if tok_rows % 96 == 0 else 1
    far = [pltpu.with_memory_space_constraint(v, pltpu.HBM) for v in (attn_out, cotangent)]
    return pl.pallas_call(
        functools.partial(product_kernel, orders, rows, owned, slabs, max(256, owned)),
        out_shape=[
            jax.ShapeDtypeStruct((features // owned, r, width), jnp.float32) for r in rows
        ],
        in_specs=[pl.BlockSpec(memory_space=pltpu.SMEM)] + [pl.BlockSpec(memory_space=pltpu.HBM)] * 2,
        out_specs=[pl.BlockSpec(memory_space=pltpu.VMEM)] * len(rows),
        scratch_shapes=[
            pltpu.VMEM((tok_rows, width), attn_out.dtype),
            pltpu.VMEM((tok_rows, features), cotangent.dtype),
            pltpu.VMEM((features, width), jnp.float32),
            pltpu.SemaphoreType.DMA((slabs,)),
            pltpu.SemaphoreType.DMA((slabs,)),
        ],
        compiler_params=pltpu.CompilerParams(vmem_limit_bytes=32 * 1024 * 1024),
        cost_estimate=pl.CostEstimate(
            flops=2 * tok_rows * width * features,
            bytes_accessed=2 * tok_rows * (width + features) + 4 * width * features,
            transcendentals=0,
        ),
    )(token_count, *far)


def swap(value, pair, reps, devices):
    pairs = [
        (r * devices + f, r * devices + (f ^ pair[r % 2]))
        for r in range(reps) for f in range(devices)
    ]
    return lax.ppermute(value, ("rep", "fsdp"), pairs)


def local(attn_out, cotangent, numer, push_weight, moment1, moment2, step_index, token_count):
    owned = numer.shape[1]
    reps, devices = lax.axis_size("rep"), lax.axis_size("fsdp")
    count = token_count[0]
    orders, rows = orders_of(devices), rows_of(owned)
    blocks = product(attn_out, cotangent, token_count, orders, rows)

    send, keep = [b[devices // 2:] for b in blocks], [b[:devices // 2] for b in blocks]
    def mate_of(value):
        def exchange(bit, v):
            return lax.ppermute(v, "rep", [(r, r ^ (1 << bit)) for r in range(reps)])

        bit_count = reps.bit_length() - 1
        if bit_count == 1:
            return exchange(0, value)
        return lax.switch(
            step_index[0] % bit_count,
            [functools.partial(exchange, b) for b in range(bit_count)],
            value,
        )

    stages = devices.bit_length() - 1
    mixed_weight = 0.75 * push_weight + 0.25 * mate_of(push_weight)
    for k in range(stages):
        got = [swap(send[c], (orders[c][0][k], orders[c][1][k]), reps, devices) for c in range(len(orders))]
        if k == 0:
            got[0], mixed_weight = lax.optimization_barrier((got[0], mixed_weight))
        for c in range(len(orders)):
            if k < stages - 1:
                half = keep[c].shape[0] // 2
                send[c] = keep[c][half:] + got[c][half:]
                keep[c] = keep[c][:half] + got[c][:half]
            else:
                keep[c] = keep[c] + got[c]
    total = jnp.concatenate(keep, axis=1)
    grad = total / count.astype(jnp.float32)
    step = step_index[0]
    t_value = (step + 1).astype(jnp.float32)
    beta_one = jnp.float32(0.9)
    beta_two = jnp.float32(0.95)
    new_moment1 = beta_one * moment1 + (1.0 - beta_one) * grad
    new_moment2 = beta_two * moment2 + (1.0 - beta_two) * grad * grad
    weight_col = push_weight[:, None, None]
    debiased = numer / weight_col
    first_hat = new_moment1 / (1.0 - jnp.power(beta_one, t_value))
    second_hat = new_moment2 / (1.0 - jnp.power(beta_two, t_value))
    update = first_hat / (jnp.sqrt(second_hat) + 1e-08) + 0.1 * debiased
    stepped = numer - 0.02 * weight_col * update

    mate_numer = mate_of(stepped)
    mixed_numer = 0.75 * stepped + 0.25 * mate_numer
    return (mixed_numer, mixed_weight, new_moment1, new_moment2)


def solution(mesh):
    placed = (
        P(("rep", "fsdp"), None),
        P(("rep", "fsdp"), None),
        P("rep", "fsdp", None),
        P("rep"),
        P("rep", "fsdp", None),
        P("rep", "fsdp", None),
        P(),
        P("rep"),
    )
    return jax.shard_map(
        local,
        mesh=mesh,
        in_specs=placed,
        out_specs=(
            P("rep", "fsdp", None),
            P("rep"),
            P("rep", "fsdp", None),
            P("rep", "fsdp", None),
        ),
        check_vma=False,
    )
```

time: 155 us -> 41.9 us (0.27)
  waiting for transfers between devices: 122 us -> 14.9 us
  starting transfers between devices: 0.04 us -> 16.8 us
  between operations: 18.1 us -> 4.57 us
  matrix products: 4.62 us -> 0 us
  blocking collectives: 4.54 us -> 0 us
  Pallas kernels: 0 us -> 3.53 us
  local copies, waits for them, and re-layouts: 2.99 us -> 0.1 us
    psum x1 -> x0, waiting for transfers between devices: 122 us -> none  [local(): whole_grad = lax.psum(partial_grad, 'fsdp')]
    ppermute x0 -> x10, starting transfers between devices: none -> 16.8 us  [the longest x8 16.1 us: swap(): return lax.ppermute(value, ('rep', 'fsdp'), pairs)]
    ppermute x0 -> x10, waiting for transfers between devices: none -> 14.9 us  [the longest x8 13.3 us: swap(): return lax.ppermute(value, ('rep', 'fsdp'), pairs)]
    dot_general x1 -> x0, matrix products: 4.62 us -> none  [local(): lax.dot_general(cotangent, masked, (((0,), (0,)), ((), ())), preferred_el...]
    pallas_call x0 -> x1, Pallas kernels: none -> 3.53 us  [product(): pl.pallas_call(functools.partial(product_kernel, orders, rows, owned, sla...]
    unnamed x1 -> x0, blocking collectives: 2.56 us -> none
    unnamed x13 -> x6, local copies, waits for them, and re-layouts: 2.4 us -> 0.01 us
    all_gather x1 -> x0, blocking collectives: 1.98 us -> none  [local(): lax.all_gather(stepped, 'rep', axis=0, tiled=True)]
  transfers between devices with their start and end apart: 1 -> 10, of which waited for: 1 -> 9; matrix products, arithmetic and copies ran while one was open for 1% -> 1% of each run, Pallas kernels for 0% -> 0%
where the time goes in v2:
time: 41.9 us; the launch traced here: 41.7 us
  starting transfers between devices  16.8 us (40%)
  waiting for transfers between devices  14.9 us (36%)
  between operations  4.57 us (11%)
  Pallas kernels  3.53 us (8%)
  other arithmetic  1.78 us (4%)
    ppermute x8, starting transfers between devices, swap(): return lax.ppermute(value, ('rep', 'fsdp'), pairs)  16.1 us
    ppermute x8, waiting for transfers between devices, swap(): return lax.ppermute(value, ('rep', 'fsdp'), pairs)  13.3 us
    pallas_call x1, Pallas kernels, product(): pl.pallas_call(functools.partial(product_kernel, orders, rows, owned, sla...  3.53 us
    ppermute x2, waiting for transfers between devices, exchange(): return lax.ppermute(v, 'rep', [(r, r ^ 1 << bit) for r in range(reps)])  1.65 us
  transfers between devices with their start and end apart: 10, of which 9 were waited for; matrix products, arithmetic and copies ran while one was open for 1% of the time, Pallas kernels for 0%

profile of v2, /device:TPU:0, one launch (start us, length us, event | category | flops | bytes accessed | tf_op | source)
XLA Modules:
  0.0 41.7 jit_solution(11721233948746439056)
XLA Ops:
  1.3 3.5 %shard_map.111 = (f32[16,32,512]{2,1,0:T(8,128)S(1)}, f32[16,32,512]{2,1,0:T(8,128)S(1)}) custom-call(s32[1]{0:T(128)S(6)} %copy.14.count, bf16[1536,512]{1,0:T(8,128)(2,1)} %attn.1, bf16[1536,1024]{1,0:T(8,128)(2,1)} %cot.1), custom_call_target="tpu_custom_call" | custom-call | flops 1610612736 | bytes 6815744 | tf_op jit(solution)/shard_map/pallas_call | solution.py:97
  4.9 3.1 %collective-permute-start = (f32[8,32,512]{2,1,0:T(8,128)S(1)}, f32[8,32,512]{2,1,0:T(8,128)S(1)}, u32[]{:S(2)}, u32[]{:S(2)}) collective-permute-start(f32[8,32,512]{2,1,0:T(8,128)S(1)} %slice.85), channel_id=1, source_target_pairs={{0,4},{1,5},{2,6},{3,7},{4,0},{5,1},{6,2},{7,3},{8,12},{9,13},{10,... | collective-permute-start | bytes 1572872 | tf_op jit(solution)/shard_map/ppermute | solution.py:125
  8.0 0.0 copy-start
  8.0 0.0 copy-start.1
  8.0 0.0 copy-start.2
  8.0 0.1 collective-permute-start.5
  8.1 0.7 %collective-permute-start.1 = (f32[1]{0:T(128)}, f32[1]{0:T(128)}, u32[]{:S(2)}, u32[]{:S(2)}) collective-permute-start(f32[1]{0:T(128)} %param.11), channel_id=1, source_target_pairs={{0,16},{16,0},{1,17},{17,1},{2,18},{18,2},{3,19},{19,3},{4,20},{20... | collective-permute-start | bytes 20 | tf_op jit(solution)/shard_map/ppermute | solution.py:138
  9.4 0.3 collective-permute-done.1
  10.4 4.7 %collective-permute-done = f32[8,32,512]{2,1,0:T(8,128)S(1)} collective-permute-done((f32[8,32,512]{2,1,0:T(8,128)S(1)}, f32[8,32,512]{2,1,0:T(8,128)S(1)}, u32[]{:S(2)}, u32[]{:S(2)}) %collective-permute-start) | collective-permute-done | bytes 524320 | tf_op jit(solution)/shard_map/ppermute | solution.py:125
  15.1 0.1 slice_add_fusion.3
  15.2 2.0 %collective-permute-start.2 = (f32[4,32,512]{2,1,0:T(8,128)S(1)}, f32[4,32,512]{2,1,0:T(8,128)S(1)}, u32[]{:S(2)}, u32[]{:S(2)}) collective-permute-start(f32[4,32,512]{2,1,0:T(8,128)S(1)} %get-tuple-element.16), channel_id=1, source_target_pairs={{0,1},{1,0},{2,3},{3,2},{4,5},{5,4},{6,7},{7,6},{8,9},{9,8},{10,11... | collective-permute-start | bytes 786440 | tf_op jit(solution)/shard_map/ppermute | solution.py:125
  17.2 3.5 %collective-permute-done.5 = f32[8,32,512]{2,1,0:T(8,128)S(1)} collective-permute-done((f32[8,32,512]{2,1,0:T(8,128)S(1)}, f32[8,32,512]{2,1,0:T(8,128)S(1)}, u32[]{:S(2)}, u32[]{:S(2)}) %collective-permute-start.5) | collective-permute-done | bytes 524320 | tf_op jit(solution)/shard_map/ppermute | solution.py:125
  20.7 0.1 slice_add_fusion.1
  20.8 2.0 %collective-permute-start.6 = (f32[4,32,512]{2,1,0:T(8,128)S(1)}, f32[4,32,512]{2,1,0:T(8,128)S(1)}, u32[]{:S(2)}, u32[]{:S(2)}) collective-permute-start(f32[4,32,512]{2,1,0:T(8,128)S(1)} %get-tuple-element.18), channel_id=1, source_target_pairs={{0,2},{1,3},{2,0},{3,1},{4,6},{5,7},{6,4},{7,5},{8,10},{9,11},{10,... | collective-permute-start | bytes 786440 | tf_op jit(solution)/shard_map/ppermute | solution.py:125
  23.6 0.7 %collective-permute-done.2 = f32[4,32,512]{2,1,0:T(8,128)S(1)} collective-permute-done((f32[4,32,512]{2,1,0:T(8,128)S(1)}, f32[4,32,512]{2,1,0:T(8,128)S(1)}, u32[]{:S(2)}, u32[]{:S(2)}) %collective-permute-start.2) | collective-permute-done | bytes 262176 | tf_op jit(solution)/shard_map/ppermute | solution.py:125
  24.3 2.7 %collective-permute-start.3 = (f32[2,32,512]{2,1,0:T(8,128)S(1)}, f32[2,32,512]{2,1,0:T(8,128)S(1)}, u32[]{:S(2)}, u32[]{:S(2)}) collective-permute-start(f32[2,32,512]{2,1,0:T(8,128)S(1)} %get-tuple-element.20), channel_id=1, source_target_pairs={{0,8},{1,9},{2,10},{3,11},{4,12},{5,13},{6,14},{7,15},{8,0},{9,1},... | collective-permute-start | bytes 393224 | tf_op jit(solution)/shard_map/ppermute | solution.py:125
  27.1 0.2 collective-permute-done.6
  27.3 2.0 %collective-permute-start.7 = (f32[2,32,512]{2,1,0:T(8,128)S(1)}, f32[2,32,512]{2,1,0:T(8,128)S(1)}, u32[]{:S(2)}, u32[]{:S(2)}) collective-permute-start(f32[2,32,512]{2,1,0:T(8,128)S(1)} %get-tuple-element.22), channel_id=1, source_target_pairs={{0,1},{1,0},{2,3},{3,2},{4,5},{5,4},{6,7},{7,6},{8,9},{9,8},{10,11... | collective-permute-start | bytes 393224 | tf_op jit(solution)/shard_map/ppermute | solution.py:125
  29.3 1.8 %collective-permute-done.3 = f32[2,32,512]{2,1,0:T(8,128)S(1)} collective-permute-done((f32[2,32,512]{2,1,0:T(8,128)S(1)}, f32[2,32,512]{2,1,0:T(8,128)S(1)}, u32[]{:S(2)}, u32[]{:S(2)}) %collective-permute-start.3) | collective-permute-done | bytes 131104 | tf_op jit(solution)/shard_map/ppermute | solution.py:125
  31.1 1.1 %collective-permute-start.4 = (f32[1,32,512]{2,1,0:T(8,128)S(1)}, f32[1,32,512]{2,1,0:T(8,128)S(1)}, u32[]{:S(2)}, u32[]{:S(2)}) collective-permute-start(f32[1,32,512]{2,1,0:T(8,128)S(1)} %slice_add_fusion.10), channel_id=1, source_target_pairs={{0,2},{1,3},{2,0},{3,1},{4,6},{5,7},{6,4},{7,5},{8,10},{9,11},{10,... | collective-permute-start | bytes 196616 | tf_op jit(solution)/shard_map/ppermute | solution.py:125
  32.2 0.1 collective-permute-done.7
  32.3 3.1 %collective-permute-start.8 = (f32[1,32,512]{2,1,0:T(8,128)S(1)}, f32[1,32,512]{2,1,0:T(8,128)S(1)}, u32[]{:S(2)}, u32[]{:S(2)}) collective-permute-start(f32[1,32,512]{2,1,0:T(8,128)S(1)} %slice_add_fusion.8), channel_id=1, source_target_pairs={{0,8},{1,9},{2,10},{3,11},{4,12},{5,13},{6,14},{7,15},{8,0},{9,1},... | collective-permute-start | bytes 196616 | tf_op jit(solution)/shard_map/ppermute | solution.py:125
  35.4 0.0 collective-permute-done.4
  35.5 2.2 %collective-permute-done.8 = f32[1,32,512]{2,1,0:T(8,128)S(1)} collective-permute-done((f32[1,32,512]{2,1,0:T(8,128)S(1)}, f32[1,32,512]{2,1,0:T(8,128)S(1)}, u32[]{:S(2)}, u32[]{:S(2)}) %collective-permute-start.8) | collective-permute-done | bytes 65568 | tf_op jit(solution)/shard_map/ppermute | solution.py:125
  37.7 0.0 copy-done
  37.7 0.0 copy-done.1
  37.7 0.0 copy-done.2
  37.7 0.8 %multiply_subtract_fusion = (f32[1,64,512]{2,1,0:T(8,128)S(1)}, f32[1,64,512]{2,1,0:T(8,128)}, f32[1,64,512]{2,1,0:T(8,128)}) fusion(f32[1,64,512]{2,1,0:T(8,128)S(1)} %copy-done, f32[]{:T(128)} %bitcast.5, f32[]{:T(128)} %bitcast.3, f32[]{:T(128)} %bitcast.2, f32[]{:T(128)} %bitcast, f32[]{:T(128)} %bitcast.1, f32[1,32,512]{2,1,0:T(8,128)S(1)} %fusion.1, ...), kind=kLoop, calls=%fused_computation.12 | loop fusion | flops 589824 | bytes 917524 | tf_op jit(solution)/shard_map/sub | solution.py:175
  38.5 0.0 collective-permute-start.9
  38.5 1.3 %collective-permute-done.9 = f32[1,64,512]{2,1,0:T(8,128)S(1)} collective-permute-done((f32[1,64,512]{2,1,0:T(8,128)S(1)}, f32[1,64,512]{2,1,0:T(8,128)S(1)}, u32[]{:S(2)}, u32[]{:S(2)}) %collective-permute-start.9) | collective-permute-done | bytes 131104 | tf_op jit(solution)/shard_map/ppermute | solution.py:138
  39.9 0.7 %multiply_add_fusion = f32[1,64,512]{2,1,0:T(8,128)} fusion(f32[1,64,512]{2,1,0:T(8,128)S(1)} %collective-permute-done.9, f32[1,64,512]{2,1,0:T(8,128)S(1)} %get-tuple-element.12), kind=kLoop, calls=%fused_computation.11 | loop fusion | flops 98304 | bytes 393216 | tf_op jit(solution)/shard_map/add | solution.py:178
  (8 shorter events, 0.2 us)
Async XLA Ops:
  4.9 10.2 %collective-permute-start = (f32[8,32,512]{2,1,0:T(8,128)S(1)}, f32[8,32,512]{2,1,0:T(8,128)S(1)}, u32[]{:S(2)}, u32[]{:S(2)}) collective-permute-start(f32[8,32,512]{2,1,0:T(8,128)S(1)} %slice.85), channel_id=1, source_target_pairs={{0,4},{1,5},{2,6},{3,7},{4,0},{5,1},{6,2},{7,3},{8,12},{9,13},{10,... | collective-permute-start | bytes 1572872 | tf_op jit(solution)/shard_map/ppermute | solution.py:125
  8.0 29.7 %copy-start = (f32[1,64,512]{2,1,0:T(8,128)S(1)}, f32[1,64,512]{2,1,0:T(8,128)}, u32[]{:S(2)}) copy-start(f32[1,64,512]{2,1,0:T(8,128)} %param.10) | copy-start | bytes 393220
  8.0 29.8 %copy-start.1 = (f32[1,64,512]{2,1,0:T(8,128)S(1)}, f32[1,64,512]{2,1,0:T(8,128)}, u32[]{:S(2)}) copy-start(f32[1,64,512]{2,1,0:T(8,128)} %param.13) | copy-start | bytes 393220
  8.0 29.8 %copy-start.2 = (f32[1,64,512]{2,1,0:T(8,128)S(1)}, f32[1,64,512]{2,1,0:T(8,128)}, u32[]{:S(2)}) copy-start(f32[1,64,512]{2,1,0:T(8,128)} %param.12) | copy-start | bytes 393220
  8.0 12.7 %collective-permute-start.5 = (f32[8,32,512]{2,1,0:T(8,128)S(1)}, f32[8,32,512]{2,1,0:T(8,128)S(1)}, u32[]{:S(2)}, u32[]{:S(2)}) collective-permute-start(f32[8,32,512]{2,1,0:T(8,128)S(1)} %slice.98), channel_id=1, source_target_pairs={{0,4},{1,5},{2,6},{3,7},{4,0},{5,1},{6,2},{7,3},{8,12},{9,13},{10,... | collective-permute-start | bytes 1572872 | tf_op jit(solution)/shard_map/ppermute | solution.py:125
  8.1 1.6 %collective-permute-start.1 = (f32[1]{0:T(128)}, f32[1]{0:T(128)}, u32[]{:S(2)}, u32[]{:S(2)}) collective-permute-start(f32[1]{0:T(128)} %param.11), channel_id=1, source_target_pairs={{0,16},{16,0},{1,17},{17,1},{2,18},{18,2},{3,19},{19,3},{4,20},{20... | collective-permute-start | bytes 20 | tf_op jit(solution)/shard_map/ppermute | solution.py:138
  15.2 9.1 %collective-permute-start.2 = (f32[4,32,512]{2,1,0:T(8,128)S(1)}, f32[4,32,512]{2,1,0:T(8,128)S(1)}, u32[]{:S(2)}, u32[]{:S(2)}) collective-permute-start(f32[4,32,512]{2,1,0:T(8,128)S(1)} %get-tuple-element.16), channel_id=1, source_target_pairs={{0,1},{1,0},{2,3},{3,2},{4,5},{5,4},{6,7},{7,6},{8,9},{9,8},{10,11... | collective-permute-start | bytes 786440 | tf_op jit(solution)/shard_map/ppermute | solution.py:125
  20.8 6.4 %collective-permute-start.6 = (f32[4,32,512]{2,1,0:T(8,128)S(1)}, f32[4,32,512]{2,1,0:T(8,128)S(1)}, u32[]{:S(2)}, u32[]{:S(2)}) collective-permute-start(f32[4,32,512]{2,1,0:T(8,128)S(1)} %get-tuple-element.18), channel_id=1, source_target_pairs={{0,2},{1,3},{2,0},{3,1},{4,6},{5,7},{6,4},{7,5},{8,10},{9,11},{10,... | collective-permute-start | bytes 786440 | tf_op jit(solution)/shard_map/ppermute | solution.py:125
  24.3 6.8 %collective-permute-start.3 = (f32[2,32,512]{2,1,0:T(8,128)S(1)}, f32[2,32,512]{2,1,0:T(8,128)S(1)}, u32[]{:S(2)}, u32[]{:S(2)}) collective-permute-start(f32[2,32,512]{2,1,0:T(8,128)S(1)} %get-tuple-element.20), channel_id=1, source_target_pairs={{0,8},{1,9},{2,10},{3,11},{4,12},{5,13},{6,14},{7,15},{8,0},{9,1},... | collective-permute-start | bytes 393224 | tf_op jit(solution)/shard_map/ppermute | solution.py:125
  27.3 5.0 %collective-permute-start.7 = (f32[2,32,512]{2,1,0:T(8,128)S(1)}, f32[2,32,512]{2,1,0:T(8,128)S(1)}, u32[]{:S(2)}, u32[]{:S(2)}) collective-permute-start(f32[2,32,512]{2,1,0:T(8,128)S(1)} %get-tuple-element.22), channel_id=1, source_target_pairs={{0,1},{1,0},{2,3},{3,2},{4,5},{5,4},{6,7},{7,6},{8,9},{9,8},{10,11... | collective-permute-start | bytes 393224 | tf_op jit(solution)/shard_map/ppermute | solution.py:125
  31.1 4.3 %collective-permute-start.4 = (f32[1,32,512]{2,1,0:T(8,128)S(1)}, f32[1,32,512]{2,1,0:T(8,128)S(1)}, u32[]{:S(2)}, u32[]{:S(2)}) collective-permute-start(f32[1,32,512]{2,1,0:T(8,128)S(1)} %slice_add_fusion.10), channel_id=1, source_target_pairs={{0,2},{1,3},{2,0},{3,1},{4,6},{5,7},{6,4},{7,5},{8,10},{9,11},{10,... | collective-permute-start | bytes 196616 | tf_op jit(solution)/shard_map/ppermute | solution.py:125
  32.3 5.3 %collective-permute-start.8 = (f32[1,32,512]{2,1,0:T(8,128)S(1)}, f32[1,32,512]{2,1,0:T(8,128)S(1)}, u32[]{:S(2)}, u32[]{:S(2)}) collective-permute-start(f32[1,32,512]{2,1,0:T(8,128)S(1)} %slice_add_fusion.8), channel_id=1, source_target_pairs={{0,8},{1,9},{2,10},{3,11},{4,12},{5,13},{6,14},{7,15},{8,0},{9,1},... | collective-permute-start | bytes 196616 | tf_op jit(solution)/shard_map/ppermute | solution.py:125
  38.5 1.3 %collective-permute-start.9 = (f32[1,64,512]{2,1,0:T(8,128)S(1)}, f32[1,64,512]{2,1,0:T(8,128)S(1)}, u32[]{:S(2)}, u32[]{:S(2)}) collective-permute-start(f32[1,64,512]{2,1,0:T(8,128)S(1)} %get-tuple-element.12), channel_id=1, source_target_pairs={{0,16},{16,0},{1,17},{17,1},{2,18},{18,2},{3,19},{19,3},{4,20},{20... | collective-permute-start | bytes 393224 | tf_op jit(solution)/shard_map/ppermute | solution.py:138

commit v3 on v2

--- a/solution.py
+++ b/solution.py
@@ -7,8 +7,8 @@
 from jax.sharding import PartitionSpec as P
 
 ORDERS = (
-    ((4, 1, 8, 2), (1, 2, 8, 4)),
-    ((4, 2, 1, 8), (2, 1, 4, 8)),
+    ((1, 2, 4, 8), (8, 2, 1, 4)),
+    ((2, 4, 8, 1), (4, 1, 2, 8)),
 )
 SHARE = 0.5
 

time: 41.9 us -> 39.8 us (0.950)
  waiting for transfers between devices: 14.9 us -> 9.37 us
  starting transfers between devices: 16.8 us -> 20.3 us
    ppermute x8, waiting for transfers between devices: 13.3 us -> 8.08 us  [swap(): return lax.ppermute(value, ('rep', 'fsdp'), pairs)]
    ppermute x8, starting transfers between devices: 16.1 us -> 19 us  [swap(): return lax.ppermute(value, ('rep', 'fsdp'), pairs)]
    ppermute x2, starting transfers between devices: 0.66 us -> 1.31 us  [exchange(): return lax.ppermute(v, 'rep', [(r, r ^ 1 << bit) for r in range(reps)])]
  transfers between devices with their start and end apart: 10 -> 10, of which waited for: 9 -> 7; matrix products, arithmetic and copies ran while one was open for 1% -> 1% of each run, Pallas kernels for 0% -> 0%
where the time goes in v3:
time: 39.8 us; the launch traced here: 39.6 us
  starting transfers between devices  20.3 us (51%)
  waiting for transfers between devices  9.37 us (24%)
  between operations  4.58 us (12%)
  Pallas kernels  3.53 us (9%)
  other arithmetic  1.78 us (4%)
    ppermute x8, starting transfers between devices, swap(): return lax.ppermute(value, ('rep', 'fsdp'), pairs)  19 us
    ppermute x8, waiting for transfers between devices, swap(): return lax.ppermute(value, ('rep', 'fsdp'), pairs)  8.08 us
    pallas_call x1, Pallas kernels, product(): pl.pallas_call(functools.partial(product_kernel, orders, rows, owned, sla...  3.53 us
    ppermute x2, starting transfers between devices, exchange(): return lax.ppermute(v, 'rep', [(r, r ^ 1 << bit) for r in range(reps)])  1.31 us
    ppermute x2, waiting for transfers between devices, exchange(): return lax.ppermute(v, 'rep', [(r, r ^ 1 << bit) for r in range(reps)])  1.29 us
    sub x1, other arithmetic, local(): stepped = numer - 0.02 * weight_col * update  0.81 us
  transfers between devices with their start and end apart: 10, of which 7 were waited for; matrix products, arithmetic and copies ran while one was open for 1% of the time, Pallas kernels for 0%

profile of v3, /device:TPU:0, one launch (start us, length us, event | category | flops | bytes accessed | tf_op | source)
XLA Modules:
  0.0 39.6 jit_solution(12877034890866711528)
XLA Ops:
  1.3 3.5 %shard_map.111 = (f32[16,32,512]{2,1,0:T(8,128)S(1)}, f32[16,32,512]{2,1,0:T(8,128)S(1)}) custom-call(s32[1]{0:T(128)S(6)} %copy.14.count, bf16[1536,512]{1,0:T(8,128)(2,1)} %attn.1, bf16[1536,1024]{1,0:T(8,128)(2,1)} %cot.1), custom_call_target="tpu_custom_call" | custom-call | flops 1610612736 | bytes 6815744 | tf_op jit(solution)/shard_map/pallas_call | solution.py:97
  4.9 3.0 %collective-permute-start = (f32[8,32,512]{2,1,0:T(8,128)S(1)}, f32[8,32,512]{2,1,0:T(8,128)S(1)}, u32[]{:S(2)}, u32[]{:S(2)}) collective-permute-start(f32[8,32,512]{2,1,0:T(8,128)S(1)} %slice.85), channel_id=1, source_target_pairs={{0,1},{1,0},{2,3},{3,2},{4,5},{5,4},{6,7},{7,6},{8,9},{9,8},{10,11... | collective-permute-start | bytes 1572872 | tf_op jit(solution)/shard_map/ppermute | solution.py:125
  7.9 0.0 copy-start
  7.9 0.0 copy-start.1
  7.9 0.0 copy-start.2
  7.9 1.6 %collective-permute-start.5 = (f32[8,32,512]{2,1,0:T(8,128)S(1)}, f32[8,32,512]{2,1,0:T(8,128)S(1)}, u32[]{:S(2)}, u32[]{:S(2)}) collective-permute-start(f32[8,32,512]{2,1,0:T(8,128)S(1)} %slice.98), channel_id=1, source_target_pairs={{0,2},{1,3},{2,0},{3,1},{4,6},{5,7},{6,4},{7,5},{8,10},{9,11},{10,... | collective-permute-start | bytes 1572872 | tf_op jit(solution)/shard_map/ppermute | solution.py:125
  9.5 0.7 %collective-permute-start.1 = (f32[1]{0:T(128)}, f32[1]{0:T(128)}, u32[]{:S(2)}, u32[]{:S(2)}) collective-permute-start(f32[1]{0:T(128)} %param.11), channel_id=1, source_target_pairs={{0,16},{16,0},{1,17},{17,1},{2,18},{18,2},{3,19},{19,3},{4,20},{20... | collective-permute-start | bytes 20 | tf_op jit(solution)/shard_map/ppermute | solution.py:138
  10.9 0.3 collective-permute-done.1
  11.9 3.1 %collective-permute-done = f32[8,32,512]{2,1,0:T(8,128)S(1)} collective-permute-done((f32[8,32,512]{2,1,0:T(8,128)S(1)}, f32[8,32,512]{2,1,0:T(8,128)S(1)}, u32[]{:S(2)}, u32[]{:S(2)}) %collective-permute-start) | collective-permute-done | bytes 524320 | tf_op jit(solution)/shard_map/ppermute | solution.py:125
  15.0 0.1 slice_add_fusion.3
  15.1 2.1 %collective-permute-start.2 = (f32[4,32,512]{2,1,0:T(8,128)S(1)}, f32[4,32,512]{2,1,0:T(8,128)S(1)}, u32[]{:S(2)}, u32[]{:S(2)}) collective-permute-start(f32[4,32,512]{2,1,0:T(8,128)S(1)} %get-tuple-element.16), channel_id=1, source_target_pairs={{0,2},{1,3},{2,0},{3,1},{4,6},{5,7},{6,4},{7,5},{8,10},{9,11},{10,... | collective-permute-start | bytes 786440 | tf_op jit(solution)/shard_map/ppermute | solution.py:125
  17.2 0.0 collective-permute-done.5
  17.2 0.1 slice_add_fusion.1
  17.3 1.6 %collective-permute-start.6 = (f32[4,32,512]{2,1,0:T(8,128)S(1)}, f32[4,32,512]{2,1,0:T(8,128)S(1)}, u32[]{:S(2)}, u32[]{:S(2)}) collective-permute-start(f32[4,32,512]{2,1,0:T(8,128)S(1)} %get-tuple-element.18), channel_id=1, source_target_pairs={{0,4},{1,5},{2,6},{3,7},{4,0},{5,1},{6,2},{7,3},{8,12},{9,13},{10,... | collective-permute-start | bytes 786440 | tf_op jit(solution)/shard_map/ppermute | solution.py:125
  19.7 1.9 %collective-permute-done.2 = f32[4,32,512]{2,1,0:T(8,128)S(1)} collective-permute-done((f32[4,32,512]{2,1,0:T(8,128)S(1)}, f32[4,32,512]{2,1,0:T(8,128)S(1)}, u32[]{:S(2)}, u32[]{:S(2)}) %collective-permute-start.2) | collective-permute-done | bytes 262176 | tf_op jit(solution)/shard_map/ppermute | solution.py:125
  21.6 2.1 %collective-permute-start.3 = (f32[2,32,512]{2,1,0:T(8,128)S(1)}, f32[2,32,512]{2,1,0:T(8,128)S(1)}, u32[]{:S(2)}, u32[]{:S(2)}) collective-permute-start(f32[2,32,512]{2,1,0:T(8,128)S(1)} %get-tuple-element.20), channel_id=1, source_target_pairs={{0,4},{1,5},{2,6},{3,7},{4,0},{5,1},{6,2},{7,3},{8,12},{9,13},{10,... | collective-permute-start | bytes 393224 | tf_op jit(solution)/shard_map/ppermute | solution.py:125
  23.8 0.2 collective-permute-done.6
  24.1 2.7 %collective-permute-start.7 = (f32[2,32,512]{2,1,0:T(8,128)S(1)}, f32[2,32,512]{2,1,0:T(8,128)S(1)}, u32[]{:S(2)}, u32[]{:S(2)}) collective-permute-start(f32[2,32,512]{2,1,0:T(8,128)S(1)} %get-tuple-element.22), channel_id=1, source_target_pairs={{0,8},{1,9},{2,10},{3,11},{4,12},{5,13},{6,14},{7,15},{8,0},{9,1},... | collective-permute-start | bytes 393224 | tf_op jit(solution)/shard_map/ppermute | solution.py:125
  26.8 0.0 collective-permute-done.3
  26.8 4.3 %collective-permute-start.4 = (f32[1,32,512]{2,1,0:T(8,128)S(1)}, f32[1,32,512]{2,1,0:T(8,128)S(1)}, u32[]{:S(2)}, u32[]{:S(2)}) collective-permute-start(f32[1,32,512]{2,1,0:T(8,128)S(1)} %slice_add_fusion.10), channel_id=1, source_target_pairs={{0,8},{1,9},{2,10},{3,11},{4,12},{5,13},{6,14},{7,15},{8,0},{9,1},... | collective-permute-start | bytes 196616 | tf_op jit(solution)/shard_map/ppermute | solution.py:125
  31.0 0.0 collective-permute-done.7
  31.1 1.5 %collective-permute-start.8 = (f32[1,32,512]{2,1,0:T(8,128)S(1)}, f32[1,32,512]{2,1,0:T(8,128)S(1)}, u32[]{:S(2)}, u32[]{:S(2)}) collective-permute-start(f32[1,32,512]{2,1,0:T(8,128)S(1)} %slice_add_fusion.8), channel_id=1, source_target_pairs={{0,1},{1,0},{2,3},{3,2},{4,5},{5,4},{6,7},{7,6},{8,9},{9,8},{10,11... | collective-permute-start | bytes 196616 | tf_op jit(solution)/shard_map/ppermute | solution.py:125
  32.6 1.5 %collective-permute-done.4 = f32[1,32,512]{2,1,0:T(8,128)S(1)} collective-permute-done((f32[1,32,512]{2,1,0:T(8,128)S(1)}, f32[1,32,512]{2,1,0:T(8,128)S(1)}, u32[]{:S(2)}, u32[]{:S(2)}) %collective-permute-start.4) | collective-permute-done | bytes 65568 | tf_op jit(solution)/shard_map/ppermute | solution.py:125
  34.1 1.3 %collective-permute-done.8 = f32[1,32,512]{2,1,0:T(8,128)S(1)} collective-permute-done((f32[1,32,512]{2,1,0:T(8,128)S(1)}, f32[1,32,512]{2,1,0:T(8,128)S(1)}, u32[]{:S(2)}, u32[]{:S(2)}) %collective-permute-start.8) | collective-permute-done | bytes 65568 | tf_op jit(solution)/shard_map/ppermute | solution.py:125
  35.4 0.0 copy-done
  35.4 0.0 copy-done.1
  35.4 0.0 copy-done.2
  35.4 0.8 %multiply_subtract_fusion = (f32[1,64,512]{2,1,0:T(8,128)S(1)}, f32[1,64,512]{2,1,0:T(8,128)}, f32[1,64,512]{2,1,0:T(8,128)}) fusion(f32[1,64,512]{2,1,0:T(8,128)S(1)} %copy-done, f32[]{:T(128)} %bitcast.5, f32[]{:T(128)} %bitcast.3, f32[]{:T(128)} %bitcast.2, f32[]{:T(128)} %bitcast, f32[]{:T(128)} %bitcast.1, f32[1,32,512]{2,1,0:T(8,128)S(1)} %fusion.1, ...), kind=kLoop, calls=%fused_computation.12 | loop fusion | flops 589824 | bytes 917524 | tf_op jit(solution)/shard_map/sub | solution.py:175
  36.3 0.6 %collective-permute-start.9 = (f32[1,64,512]{2,1,0:T(8,128)S(1)}, f32[1,64,512]{2,1,0:T(8,128)S(1)}, u32[]{:S(2)}, u32[]{:S(2)}) collective-permute-start(f32[1,64,512]{2,1,0:T(8,128)S(1)} %get-tuple-element.12), channel_id=1, source_target_pairs={{0,16},{16,0},{1,17},{17,1},{2,18},{18,2},{3,19},{19,3},{4,20},{20... | collective-permute-start | bytes 393224 | tf_op jit(solution)/shard_map/ppermute | solution.py:138
  36.8 1.0 %collective-permute-done.9 = f32[1,64,512]{2,1,0:T(8,128)S(1)} collective-permute-done((f32[1,64,512]{2,1,0:T(8,128)S(1)}, f32[1,64,512]{2,1,0:T(8,128)S(1)}, u32[]{:S(2)}, u32[]{:S(2)}) %collective-permute-start.9) | collective-permute-done | bytes 131104 | tf_op jit(solution)/shard_map/ppermute | solution.py:138
  37.8 0.7 %multiply_add_fusion = f32[1,64,512]{2,1,0:T(8,128)} fusion(f32[1,64,512]{2,1,0:T(8,128)S(1)} %collective-permute-done.9, f32[1,64,512]{2,1,0:T(8,128)S(1)} %get-tuple-element.12), kind=kLoop, calls=%fused_computation.11 | loop fusion | flops 98304 | bytes 393216 | tf_op jit(solution)/shard_map/add | solution.py:178
  (8 shorter events, 0.2 us)
Async XLA Ops:
  4.9 10.2 %collective-permute-start = (f32[8,32,512]{2,1,0:T(8,128)S(1)}, f32[8,32,512]{2,1,0:T(8,128)S(1)}, u32[]{:S(2)}, u32[]{:S(2)}) collective-permute-start(f32[8,32,512]{2,1,0:T(8,128)S(1)} %slice.85), channel_id=1, source_target_pairs={{0,1},{1,0},{2,3},{3,2},{4,5},{5,4},{6,7},{7,6},{8,9},{9,8},{10,11... | collective-permute-start | bytes 1572872 | tf_op jit(solution)/shard_map/ppermute | solution.py:125
  7.9 27.5 %copy-start = (f32[1,64,512]{2,1,0:T(8,128)S(1)}, f32[1,64,512]{2,1,0:T(8,128)}, u32[]{:S(2)}) copy-start(f32[1,64,512]{2,1,0:T(8,128)} %param.10) | copy-start | bytes 393220
  7.9 27.6 %copy-start.1 = (f32[1,64,512]{2,1,0:T(8,128)S(1)}, f32[1,64,512]{2,1,0:T(8,128)}, u32[]{:S(2)}) copy-start(f32[1,64,512]{2,1,0:T(8,128)} %param.13) | copy-start | bytes 393220
  7.9 27.6 %copy-start.2 = (f32[1,64,512]{2,1,0:T(8,128)S(1)}, f32[1,64,512]{2,1,0:T(8,128)}, u32[]{:S(2)}) copy-start(f32[1,64,512]{2,1,0:T(8,128)} %param.12) | copy-start | bytes 393220
  7.9 9.3 %collective-permute-start.5 = (f32[8,32,512]{2,1,0:T(8,128)S(1)}, f32[8,32,512]{2,1,0:T(8,128)S(1)}, u32[]{:S(2)}, u32[]{:S(2)}) collective-permute-start(f32[8,32,512]{2,1,0:T(8,128)S(1)} %slice.98), channel_id=1, source_target_pairs={{0,2},{1,3},{2,0},{3,1},{4,6},{5,7},{6,4},{7,5},{8,10},{9,11},{10,... | collective-permute-start | bytes 1572872 | tf_op jit(solution)/shard_map/ppermute | solution.py:125
  9.5 1.7 %collective-permute-start.1 = (f32[1]{0:T(128)}, f32[1]{0:T(128)}, u32[]{:S(2)}, u32[]{:S(2)}) collective-permute-start(f32[1]{0:T(128)} %param.11), channel_id=1, source_target_pairs={{0,16},{16,0},{1,17},{17,1},{2,18},{18,2},{3,19},{19,3},{4,20},{20... | collective-permute-start | bytes 20 | tf_op jit(solution)/shard_map/ppermute | solution.py:138
  15.1 6.5 %collective-permute-start.2 = (f32[4,32,512]{2,1,0:T(8,128)S(1)}, f32[4,32,512]{2,1,0:T(8,128)S(1)}, u32[]{:S(2)}, u32[]{:S(2)}) collective-permute-start(f32[4,32,512]{2,1,0:T(8,128)S(1)} %get-tuple-element.16), channel_id=1, source_target_pairs={{0,2},{1,3},{2,0},{3,1},{4,6},{5,7},{6,4},{7,5},{8,10},{9,11},{10,... | collective-permute-start | bytes 786440 | tf_op jit(solution)/shard_map/ppermute | solution.py:125
  17.3 6.7 %collective-permute-start.6 = (f32[4,32,512]{2,1,0:T(8,128)S(1)}, f32[4,32,512]{2,1,0:T(8,128)S(1)}, u32[]{:S(2)}, u32[]{:S(2)}) collective-permute-start(f32[4,32,512]{2,1,0:T(8,128)S(1)} %get-tuple-element.18), channel_id=1, source_target_pairs={{0,4},{1,5},{2,6},{3,7},{4,0},{5,1},{6,2},{7,3},{8,12},{9,13},{10,... | collective-permute-start | bytes 786440 | tf_op jit(solution)/shard_map/ppermute | solution.py:125
  21.6 5.1 %collective-permute-start.3 = (f32[2,32,512]{2,1,0:T(8,128)S(1)}, f32[2,32,512]{2,1,0:T(8,128)S(1)}, u32[]{:S(2)}, u32[]{:S(2)}) collective-permute-start(f32[2,32,512]{2,1,0:T(8,128)S(1)} %get-tuple-element.20), channel_id=1, source_target_pairs={{0,4},{1,5},{2,6},{3,7},{4,0},{5,1},{6,2},{7,3},{8,12},{9,13},{10,... | collective-permute-start | bytes 393224 | tf_op jit(solution)/shard_map/ppermute | solution.py:125
  24.1 7.0 %collective-permute-start.7 = (f32[2,32,512]{2,1,0:T(8,128)S(1)}, f32[2,32,512]{2,1,0:T(8,128)S(1)}, u32[]{:S(2)}, u32[]{:S(2)}) collective-permute-start(f32[2,32,512]{2,1,0:T(8,128)S(1)} %get-tuple-element.22), channel_id=1, source_target_pairs={{0,8},{1,9},{2,10},{3,11},{4,12},{5,13},{6,14},{7,15},{8,0},{9,1},... | collective-permute-start | bytes 393224 | tf_op jit(solution)/shard_map/ppermute | solution.py:125
  26.8 7.3 %collective-permute-start.4 = (f32[1,32,512]{2,1,0:T(8,128)S(1)}, f32[1,32,512]{2,1,0:T(8,128)S(1)}, u32[]{:S(2)}, u32[]{:S(2)}) collective-permute-start(f32[1,32,512]{2,1,0:T(8,128)S(1)} %slice_add_fusion.10), channel_id=1, source_target_pairs={{0,8},{1,9},{2,10},{3,11},{4,12},{5,13},{6,14},{7,15},{8,0},{9,1},... | collective-permute-start | bytes 196616 | tf_op jit(solution)/shard_map/ppermute | solution.py:125
  31.1 4.3 %collective-permute-start.8 = (f32[1,32,512]{2,1,0:T(8,128)S(1)}, f32[1,32,512]{2,1,0:T(8,128)S(1)}, u32[]{:S(2)}, u32[]{:S(2)}) collective-permute-start(f32[1,32,512]{2,1,0:T(8,128)S(1)} %slice_add_fusion.8), channel_id=1, source_target_pairs={{0,1},{1,0},{2,3},{3,2},{4,5},{5,4},{6,7},{7,6},{8,9},{9,8},{10,11... | collective-permute-start | bytes 196616 | tf_op jit(solution)/shard_map/ppermute | solution.py:125
  36.3 1.6 %collective-permute-start.9 = (f32[1,64,512]{2,1,0:T(8,128)S(1)}, f32[1,64,512]{2,1,0:T(8,128)S(1)}, u32[]{:S(2)}, u32[]{:S(2)}) collective-permute-start(f32[1,64,512]{2,1,0:T(8,128)S(1)} %get-tuple-element.12), channel_id=1, source_target_pairs={{0,16},{16,0},{1,17},{17,1},{2,18},{18,2},{3,19},{19,3},{4,20},{20... | collective-permute-start | bytes 393224 | tf_op jit(solution)/shard_map/ppermute | solution.py:138

commit v4 on v3

--- a/solution.py
+++ b/solution.py
@@ -7,8 +7,8 @@
 from jax.sharding import PartitionSpec as P
 
 ORDERS = (
-    ((1, 2, 4, 8), (8, 2, 1, 4)),
-    ((2, 4, 8, 1), (4, 1, 2, 8)),
+    ((1, 2, 4, 8), (4, 1, 2, 8)),
+    ((2, 4, 1, 8), (8, 2, 1, 4)),
 )
 SHARE = 0.5
 
@@ -67,7 +67,11 @@
     for k, span in enumerate(spans):
         attn_in[k].wait()
 
-        @pl.when(live < (k + 1) * depth)
+        @pl.when(live <= k * depth)
+        def _():
+            attn_v[span] = jnp.zeros((depth, width), attn_v.dtype)
+
+        @pl.when((live > k * depth) & (live < (k + 1) * depth))
         def _():
             position = k * depth + lax.broadcasted_iota(jnp.int32, (depth, width), 0)
             kept = jnp.where(position < live, attn_v[span].astype(jnp.float32), 0.0)

time: 39.8 us -> 39.9 us (level)
  waiting for transfers between devices: 9.37 us -> 10.7 us
  starting transfers between devices: 20.3 us -> 19 us
    ppermute x8, waiting for transfers between devices: 8.08 us -> 9.43 us  [swap(): return lax.ppermute(value, ('rep', 'fsdp'), pairs)]
    ppermute x8, starting transfers between devices: 19 us -> 18 us  [swap(): return lax.ppermute(value, ('rep', 'fsdp'), pairs)]
where the time goes in v4:
time: 39.9 us; the launch traced here: 39.7 us
  starting transfers between devices  19 us (48%)
  waiting for transfers between devices  10.7 us (27%)
  between operations  4.58 us (11%)
  Pallas kernels  3.53 us (9%)
  other arithmetic  1.78 us (4%)
    ppermute x8, starting transfers between devices, swap(): return lax.ppermute(value, ('rep', 'fsdp'), pairs)  18 us
    ppermute x8, waiting for transfers between devices, swap(): return lax.ppermute(value, ('rep', 'fsdp'), pairs)  9.43 us
    pallas_call x1, Pallas kernels, product(): pl.pallas_call(functools.partial(product_kernel, orders, rows, owned, sla...  3.53 us
    ppermute x2, waiting for transfers between devices, exchange(): return lax.ppermute(v, 'rep', [(r, r ^ 1 << bit) for r in range(reps)])  1.29 us
    ppermute x2, starting transfers between devices, exchange(): return lax.ppermute(v, 'rep', [(r, r ^ 1 << bit) for r in range(reps)])  0.98 us
    sub x1, other arithmetic, local(): stepped = numer - 0.02 * weight_col * update  0.81 us
  transfers between devices with their start and end apart: 10, of which 7 were waited for; matrix products, arithmetic and copies ran while one was open for 1% of the time, Pallas kernels for 0%

profile of v4, /device:TPU:0, one launch (start us, length us, event | category | flops | bytes accessed | tf_op | source)
XLA Modules:
  0.0 39.7 jit_solution(2631451350561039967)
XLA Ops:
  1.3 3.5 %shard_map.111 = (f32[16,32,512]{2,1,0:T(8,128)S(1)}, f32[16,32,512]{2,1,0:T(8,128)S(1)}) custom-call(s32[1]{0:T(128)S(6)} %copy.14.count, bf16[1536,512]{1,0:T(8,128)(2,1)} %attn.1, bf16[1536,1024]{1,0:T(8,128)(2,1)} %cot.1), custom_call_target="tpu_custom_call" | custom-call | flops 1610612736 | bytes 6815744 | tf_op jit(solution)/shard_map/pallas_call | solution.py:101
  4.9 3.0 %collective-permute-start = (f32[8,32,512]{2,1,0:T(8,128)S(1)}, f32[8,32,512]{2,1,0:T(8,128)S(1)}, u32[]{:S(2)}, u32[]{:S(2)}) collective-permute-start(f32[8,32,512]{2,1,0:T(8,128)S(1)} %slice.85), channel_id=1, source_target_pairs={{0,1},{1,0},{2,3},{3,2},{4,5},{5,4},{6,7},{7,6},{8,9},{9,8},{10,11... | collective-permute-start | bytes 1572872 | tf_op jit(solution)/shard_map/ppermute | solution.py:129
  7.9 0.0 copy-start
  7.9 0.0 copy-start.1
  7.9 0.0 copy-start.2
  7.9 1.6 %collective-permute-start.5 = (f32[8,32,512]{2,1,0:T(8,128)S(1)}, f32[8,32,512]{2,1,0:T(8,128)S(1)}, u32[]{:S(2)}, u32[]{:S(2)}) collective-permute-start(f32[8,32,512]{2,1,0:T(8,128)S(1)} %slice.98), channel_id=1, source_target_pairs={{0,2},{1,3},{2,0},{3,1},{4,6},{5,7},{6,4},{7,5},{8,10},{9,11},{10,... | collective-permute-start | bytes 1572872 | tf_op jit(solution)/shard_map/ppermute | solution.py:129
  9.5 0.5 %collective-permute-start.1 = (f32[1]{0:T(128)}, f32[1]{0:T(128)}, u32[]{:S(2)}, u32[]{:S(2)}) collective-permute-start(f32[1]{0:T(128)} %param.11), channel_id=1, source_target_pairs={{0,16},{16,0},{1,17},{17,1},{2,18},{18,2},{3,19},{19,3},{4,20},{20... | collective-permute-start | bytes 20 | tf_op jit(solution)/shard_map/ppermute | solution.py:142
  10.7 0.3 collective-permute-done.1
  11.7 3.4 %collective-permute-done = f32[8,32,512]{2,1,0:T(8,128)S(1)} collective-permute-done((f32[8,32,512]{2,1,0:T(8,128)S(1)}, f32[8,32,512]{2,1,0:T(8,128)S(1)}, u32[]{:S(2)}, u32[]{:S(2)}) %collective-permute-start) | collective-permute-done | bytes 524320 | tf_op jit(solution)/shard_map/ppermute | solution.py:129
  15.0 0.1 slice_add_fusion.3
  15.1 2.1 %collective-permute-start.2 = (f32[4,32,512]{2,1,0:T(8,128)S(1)}, f32[4,32,512]{2,1,0:T(8,128)S(1)}, u32[]{:S(2)}, u32[]{:S(2)}) collective-permute-start(f32[4,32,512]{2,1,0:T(8,128)S(1)} %get-tuple-element.16), channel_id=1, source_target_pairs={{0,2},{1,3},{2,0},{3,1},{4,6},{5,7},{6,4},{7,5},{8,10},{9,11},{10,... | collective-permute-start | bytes 786440 | tf_op jit(solution)/shard_map/ppermute | solution.py:129
  17.2 0.0 collective-permute-done.5
  17.2 0.1 slice_add_fusion.1
  17.3 1.6 %collective-permute-start.6 = (f32[4,32,512]{2,1,0:T(8,128)S(1)}, f32[4,32,512]{2,1,0:T(8,128)S(1)}, u32[]{:S(2)}, u32[]{:S(2)}) collective-permute-start(f32[4,32,512]{2,1,0:T(8,128)S(1)} %get-tuple-element.18), channel_id=1, source_target_pairs={{0,4},{1,5},{2,6},{3,7},{4,0},{5,1},{6,2},{7,3},{8,12},{9,13},{10,... | collective-permute-start | bytes 786440 | tf_op jit(solution)/shard_map/ppermute | solution.py:129
  19.7 1.9 %collective-permute-done.2 = f32[4,32,512]{2,1,0:T(8,128)S(1)} collective-permute-done((f32[4,32,512]{2,1,0:T(8,128)S(1)}, f32[4,32,512]{2,1,0:T(8,128)S(1)}, u32[]{:S(2)}, u32[]{:S(2)}) %collective-permute-start.2) | collective-permute-done | bytes 262176 | tf_op jit(solution)/shard_map/ppermute | solution.py:129
  21.6 2.1 %collective-permute-start.3 = (f32[2,32,512]{2,1,0:T(8,128)S(1)}, f32[2,32,512]{2,1,0:T(8,128)S(1)}, u32[]{:S(2)}, u32[]{:S(2)}) collective-permute-start(f32[2,32,512]{2,1,0:T(8,128)S(1)} %get-tuple-element.20), channel_id=1, source_target_pairs={{0,4},{1,5},{2,6},{3,7},{4,0},{5,1},{6,2},{7,3},{8,12},{9,13},{10,... | collective-permute-start | bytes 393224 | tf_op jit(solution)/shard_map/ppermute | solution.py:129
  23.8 0.3 collective-permute-done.6
  24.1 1.6 %collective-permute-start.7 = (f32[2,32,512]{2,1,0:T(8,128)S(1)}, f32[2,32,512]{2,1,0:T(8,128)S(1)}, u32[]{:S(2)}, u32[]{:S(2)}) collective-permute-start(f32[2,32,512]{2,1,0:T(8,128)S(1)} %get-tuple-element.22), channel_id=1, source_target_pairs={{0,1},{1,0},{2,3},{3,2},{4,5},{5,4},{6,7},{7,6},{8,9},{9,8},{10,11... | collective-permute-start | bytes 393224 | tf_op jit(solution)/shard_map/ppermute | solution.py:129
  25.6 1.1 %collective-permute-done.3 = f32[2,32,512]{2,1,0:T(8,128)S(1)} collective-permute-done((f32[2,32,512]{2,1,0:T(8,128)S(1)}, f32[2,32,512]{2,1,0:T(8,128)S(1)}, u32[]{:S(2)}, u32[]{:S(2)}) %collective-permute-start.3) | collective-permute-done | bytes 131104 | tf_op jit(solution)/shard_map/ppermute | solution.py:129
  26.7 3.2 %collective-permute-start.4 = (f32[1,32,512]{2,1,0:T(8,128)S(1)}, f32[1,32,512]{2,1,0:T(8,128)S(1)}, u32[]{:S(2)}, u32[]{:S(2)}) collective-permute-start(f32[1,32,512]{2,1,0:T(8,128)S(1)} %slice_add_fusion.10), channel_id=1, source_target_pairs={{0,8},{1,9},{2,10},{3,11},{4,12},{5,13},{6,14},{7,15},{8,0},{9,1},... | collective-permute-start | bytes 196616 | tf_op jit(solution)/shard_map/ppermute | solution.py:129
  29.9 0.0 collective-permute-done.7
  29.9 2.8 %collective-permute-start.8 = (f32[1,32,512]{2,1,0:T(8,128)S(1)}, f32[1,32,512]{2,1,0:T(8,128)S(1)}, u32[]{:S(2)}, u32[]{:S(2)}) collective-permute-start(f32[1,32,512]{2,1,0:T(8,128)S(1)} %slice_add_fusion.8), channel_id=1, source_target_pairs={{0,8},{1,9},{2,10},{3,11},{4,12},{5,13},{6,14},{7,15},{8,0},{9,1},... | collective-permute-start | bytes 196616 | tf_op jit(solution)/shard_map/ppermute | solution.py:129
  32.7 0.0 collective-permute-done.4
  32.7 2.8 %collective-permute-done.8 = f32[1,32,512]{2,1,0:T(8,128)S(1)} collective-permute-done((f32[1,32,512]{2,1,0:T(8,128)S(1)}, f32[1,32,512]{2,1,0:T(8,128)S(1)}, u32[]{:S(2)}, u32[]{:S(2)}) %collective-permute-start.8) | collective-permute-done | bytes 65568 | tf_op jit(solution)/shard_map/ppermute | solution.py:129
  35.6 0.0 copy-done
  35.6 0.0 copy-done.1
  35.6 0.0 copy-done.2
  35.6 0.8 %multiply_subtract_fusion = (f32[1,64,512]{2,1,0:T(8,128)S(1)}, f32[1,64,512]{2,1,0:T(8,128)}, f32[1,64,512]{2,1,0:T(8,128)}) fusion(f32[1,64,512]{2,1,0:T(8,128)S(1)} %copy-done, f32[]{:T(128)} %bitcast.5, f32[]{:T(128)} %bitcast.3, f32[]{:T(128)} %bitcast.2, f32[]{:T(128)} %bitcast, f32[]{:T(128)} %bitcast.1, f32[1,32,512]{2,1,0:T(8,128)S(1)} %fusion.1, ...), kind=kLoop, calls=%fused_computation.12 | loop fusion | flops 589824 | bytes 917524 | tf_op jit(solution)/shard_map/sub | solution.py:179
  36.4 0.5 %collective-permute-start.9 = (f32[1,64,512]{2,1,0:T(8,128)S(1)}, f32[1,64,512]{2,1,0:T(8,128)S(1)}, u32[]{:S(2)}, u32[]{:S(2)}) collective-permute-start(f32[1,64,512]{2,1,0:T(8,128)S(1)} %get-tuple-element.12), channel_id=1, source_target_pairs={{0,16},{16,0},{1,17},{17,1},{2,18},{18,2},{3,19},{19,3},{4,20},{20... | collective-permute-start | bytes 393224 | tf_op jit(solution)/shard_map/ppermute | solution.py:142
  36.9 1.0 %collective-permute-done.9 = f32[1,64,512]{2,1,0:T(8,128)S(1)} collective-permute-done((f32[1,64,512]{2,1,0:T(8,128)S(1)}, f32[1,64,512]{2,1,0:T(8,128)S(1)}, u32[]{:S(2)}, u32[]{:S(2)}) %collective-permute-start.9) | collective-permute-done | bytes 131104 | tf_op jit(solution)/shard_map/ppermute | solution.py:142
  37.9 0.7 %multiply_add_fusion = f32[1,64,512]{2,1,0:T(8,128)} fusion(f32[1,64,512]{2,1,0:T(8,128)S(1)} %collective-permute-done.9, f32[1,64,512]{2,1,0:T(8,128)S(1)} %get-tuple-element.12), kind=kLoop, calls=%fused_computation.11 | loop fusion | flops 98304 | bytes 393216 | tf_op jit(solution)/shard_map/add | solution.py:182
  (8 shorter events, 0.2 us)
Async XLA Ops:
  4.9 10.2 %collective-permute-start = (f32[8,32,512]{2,1,0:T(8,128)S(1)}, f32[8,32,512]{2,1,0:T(8,128)S(1)}, u32[]{:S(2)}, u32[]{:S(2)}) collective-permute-start(f32[8,32,512]{2,1,0:T(8,128)S(1)} %slice.85), channel_id=1, source_target_pairs={{0,1},{1,0},{2,3},{3,2},{4,5},{5,4},{6,7},{7,6},{8,9},{9,8},{10,11... | collective-permute-start | bytes 1572872 | tf_op jit(solution)/shard_map/ppermute | solution.py:129
  7.9 27.7 %copy-start = (f32[1,64,512]{2,1,0:T(8,128)S(1)}, f32[1,64,512]{2,1,0:T(8,128)}, u32[]{:S(2)}) copy-start(f32[1,64,512]{2,1,0:T(8,128)} %param.10) | copy-start | bytes 393220
  7.9 27.7 %copy-start.1 = (f32[1,64,512]{2,1,0:T(8,128)S(1)}, f32[1,64,512]{2,1,0:T(8,128)}, u32[]{:S(2)}) copy-start(f32[1,64,512]{2,1,0:T(8,128)} %param.13) | copy-start | bytes 393220
  7.9 27.7 %copy-start.2 = (f32[1,64,512]{2,1,0:T(8,128)S(1)}, f32[1,64,512]{2,1,0:T(8,128)}, u32[]{:S(2)}) copy-start(f32[1,64,512]{2,1,0:T(8,128)} %param.12) | copy-start | bytes 393220
  7.9 9.3 %collective-permute-start.5 = (f32[8,32,512]{2,1,0:T(8,128)S(1)}, f32[8,32,512]{2,1,0:T(8,128)S(1)}, u32[]{:S(2)}, u32[]{:S(2)}) collective-permute-start(f32[8,32,512]{2,1,0:T(8,128)S(1)} %slice.98), channel_id=1, source_target_pairs={{0,2},{1,3},{2,0},{3,1},{4,6},{5,7},{6,4},{7,5},{8,10},{9,11},{10,... | collective-permute-start | bytes 1572872 | tf_op jit(solution)/shard_map/ppermute | solution.py:129
  9.5 1.5 %collective-permute-start.1 = (f32[1]{0:T(128)}, f32[1]{0:T(128)}, u32[]{:S(2)}, u32[]{:S(2)}) collective-permute-start(f32[1]{0:T(128)} %param.11), channel_id=1, source_target_pairs={{0,16},{16,0},{1,17},{17,1},{2,18},{18,2},{3,19},{19,3},{4,20},{20... | collective-permute-start | bytes 20 | tf_op jit(solution)/shard_map/ppermute | solution.py:142
  15.1 6.5 %collective-permute-start.2 = (f32[4,32,512]{2,1,0:T(8,128)S(1)}, f32[4,32,512]{2,1,0:T(8,128)S(1)}, u32[]{:S(2)}, u32[]{:S(2)}) collective-permute-start(f32[4,32,512]{2,1,0:T(8,128)S(1)} %get-tuple-element.16), channel_id=1, source_target_pairs={{0,2},{1,3},{2,0},{3,1},{4,6},{5,7},{6,4},{7,5},{8,10},{9,11},{10,... | collective-permute-start | bytes 786440 | tf_op jit(solution)/shard_map/ppermute | solution.py:129
  17.3 6.7 %collective-permute-start.6 = (f32[4,32,512]{2,1,0:T(8,128)S(1)}, f32[4,32,512]{2,1,0:T(8,128)S(1)}, u32[]{:S(2)}, u32[]{:S(2)}) collective-permute-start(f32[4,32,512]{2,1,0:T(8,128)S(1)} %get-tuple-element.18), channel_id=1, source_target_pairs={{0,4},{1,5},{2,6},{3,7},{4,0},{5,1},{6,2},{7,3},{8,12},{9,13},{10,... | collective-permute-start | bytes 786440 | tf_op jit(solution)/shard_map/ppermute | solution.py:129
  21.6 5.1 %collective-permute-start.3 = (f32[2,32,512]{2,1,0:T(8,128)S(1)}, f32[2,32,512]{2,1,0:T(8,128)S(1)}, u32[]{:S(2)}, u32[]{:S(2)}) collective-permute-start(f32[2,32,512]{2,1,0:T(8,128)S(1)} %get-tuple-element.20), channel_id=1, source_target_pairs={{0,4},{1,5},{2,6},{3,7},{4,0},{5,1},{6,2},{7,3},{8,12},{9,13},{10,... | collective-permute-start | bytes 393224 | tf_op jit(solution)/shard_map/ppermute | solution.py:129
  24.1 5.9 %collective-permute-start.7 = (f32[2,32,512]{2,1,0:T(8,128)S(1)}, f32[2,32,512]{2,1,0:T(8,128)S(1)}, u32[]{:S(2)}, u32[]{:S(2)}) collective-permute-start(f32[2,32,512]{2,1,0:T(8,128)S(1)} %get-tuple-element.22), channel_id=1, source_target_pairs={{0,1},{1,0},{2,3},{3,2},{4,5},{5,4},{6,7},{7,6},{8,9},{9,8},{10,11... | collective-permute-start | bytes 393224 | tf_op jit(solution)/shard_map/ppermute | solution.py:129
  26.7 6.0 %collective-permute-start.4 = (f32[1,32,512]{2,1,0:T(8,128)S(1)}, f32[1,32,512]{2,1,0:T(8,128)S(1)}, u32[]{:S(2)}, u32[]{:S(2)}) collective-permute-start(f32[1,32,512]{2,1,0:T(8,128)S(1)} %slice_add_fusion.10), channel_id=1, source_target_pairs={{0,8},{1,9},{2,10},{3,11},{4,12},{5,13},{6,14},{7,15},{8,0},{9,1},... | collective-permute-start | bytes 196616 | tf_op jit(solution)/shard_map/ppermute | solution.py:129
  29.9 5.6 %collective-permute-start.8 = (f32[1,32,512]{2,1,0:T(8,128)S(1)}, f32[1,32,512]{2,1,0:T(8,128)S(1)}, u32[]{:S(2)}, u32[]{:S(2)}) collective-permute-start(f32[1,32,512]{2,1,0:T(8,128)S(1)} %slice_add_fusion.8), channel_id=1, source_target_pairs={{0,8},{1,9},{2,10},{3,11},{4,12},{5,13},{6,14},{7,15},{8,0},{9,1},... | collective-permute-start | bytes 196616 | tf_op jit(solution)/shard_map/ppermute | solution.py:129
  36.4 1.4 %collective-permute-start.9 = (f32[1,64,512]{2,1,0:T(8,128)S(1)}, f32[1,64,512]{2,1,0:T(8,128)S(1)}, u32[]{:S(2)}, u32[]{:S(2)}) collective-permute-start(f32[1,64,512]{2,1,0:T(8,128)S(1)} %get-tuple-element.12), channel_id=1, source_target_pairs={{0,16},{16,0},{1,17},{17,1},{2,18},{18,2},{3,19},{19,3},{4,20},{20... | collective-permute-start | bytes 393224 | tf_op jit(solution)/shard_map/ppermute | solution.py:142

commit v5 on v3

--- a/solution.py
+++ b/solution.py
@@ -148,10 +148,17 @@
 
     stages = devices.bit_length() - 1
     mixed_weight = 0.75 * push_weight + 0.25 * mate_of(push_weight)
+    t_value = (step_index[0] + 1).astype(jnp.float32)
+    beta_one = jnp.float32(0.9)
+    beta_two = jnp.float32(0.95)
+    one = 1.0 - jnp.power(beta_one, t_value)
+    two = 1.0 - jnp.power(beta_two, t_value)
     for k in range(stages):
         got = [swap(send[c], (orders[c][0][k], orders[c][1][k]), reps, devices) for c in range(len(orders))]
         if k == 0:
-            got[0], mixed_weight = lax.optimization_barrier((got[0], mixed_weight))
+            got[0], mixed_weight, one, two = lax.optimization_barrier(
+                (got[0], mixed_weight, one, two)
+            )
         for c in range(len(orders)):
             if k < stages - 1:
                 half = keep[c].shape[0] // 2
@@ -161,16 +168,12 @@
                 keep[c] = keep[c] + got[c]
     total = jnp.concatenate(keep, axis=1)
     grad = total / count.astype(jnp.float32)
-    step = step_index[0]
-    t_value = (step + 1).astype(jnp.float32)
-    beta_one = jnp.float32(0.9)
-    beta_two = jnp.float32(0.95)
     new_moment1 = beta_one * moment1 + (1.0 - beta_one) * grad
     new_moment2 = beta_two * moment2 + (1.0 - beta_two) * grad * grad
     weight_col = push_weight[:, None, None]
     debiased = numer / weight_col
-    first_hat = new_moment1 / (1.0 - jnp.power(beta_one, t_value))
-    second_hat = new_moment2 / (1.0 - jnp.power(beta_two, t_value))
+    first_hat = new_moment1 / one
+    second_hat = new_moment2 / two
     update = first_hat / (jnp.sqrt(second_hat) + 1e-08) + 0.1 * debiased
     stepped = numer - 0.02 * weight_col * update
 

time: 39.8 us -> 39.8 us (level)
  waiting for transfers between devices: 9.37 us -> 10.2 us
  starting transfers between devices: 20.3 us -> 19.6 us
    ppermute x8, waiting for transfers between devices: 8.08 us -> 9.19 us  [swap(): return lax.ppermute(value, ('rep', 'fsdp'), pairs)]
where the time goes in v5:
time: 39.8 us; the launch traced here: 39.6 us
  starting transfers between devices  19.6 us (49%)
  waiting for transfers between devices  10.2 us (26%)
  between operations  4.45 us (11%)
  Pallas kernels  3.53 us (9%)
  other arithmetic  1.78 us (4%)
    ppermute x8, starting transfers between devices, swap(): return lax.ppermute(value, ('rep', 'fsdp'), pairs)  18.6 us
    ppermute x8, waiting for transfers between devices, swap(): return lax.ppermute(value, ('rep', 'fsdp'), pairs)  9.19 us
    pallas_call x1, Pallas kernels, product(): pl.pallas_call(functools.partial(product_kernel, orders, rows, owned, sla...  3.53 us
    ppermute x2, starting transfers between devices, exchange(): return lax.ppermute(v, 'rep', [(r, r ^ 1 << bit) for r in range(reps)])  1 us
    ppermute x2, waiting for transfers between devices, exchange(): return lax.ppermute(v, 'rep', [(r, r ^ 1 << bit) for r in range(reps)])  0.99 us
    sub x1, other arithmetic, local(): stepped = numer - 0.02 * weight_col * update  0.81 us
  transfers between devices with their start and end apart: 10, of which 7 were waited for; matrix products, arithmetic and copies ran while one was open for 1% of the time, Pallas kernels for 0%

profile of v5, /device:TPU:0, one launch (start us, length us, event | category | flops | bytes accessed | tf_op | source)
XLA Modules:
  0.0 39.6 jit_solution(10960216922975860551)
XLA Ops:
  1.3 3.5 %shard_map.111 = (f32[16,32,512]{2,1,0:T(8,128)S(1)}, f32[16,32,512]{2,1,0:T(8,128)S(1)}) custom-call(s32[1]{0:T(128)S(6)} %copy.14.count, bf16[1536,512]{1,0:T(8,128)(2,1)} %attn.1, bf16[1536,1024]{1,0:T(8,128)(2,1)} %cot.1), custom_call_target="tpu_custom_call" | custom-call | flops 1610612736 | bytes 6815744 | tf_op jit(solution)/shard_map/pallas_call | solution.py:97
  4.9 3.0 %collective-permute-start = (f32[8,32,512]{2,1,0:T(8,128)S(1)}, f32[8,32,512]{2,1,0:T(8,128)S(1)}, u32[]{:S(2)}, u32[]{:S(2)}) collective-permute-start(f32[8,32,512]{2,1,0:T(8,128)S(1)} %slice.85), channel_id=1, source_target_pairs={{0,1},{1,0},{2,3},{3,2},{4,5},{5,4},{6,7},{7,6},{8,9},{9,8},{10,11... | collective-permute-start | bytes 1572872 | tf_op jit(solution)/shard_map/ppermute | solution.py:125
  7.9 0.0 copy-start
  7.9 0.0 copy-start.1
  7.9 0.0 copy-start.2
  7.9 1.6 %collective-permute-start.5 = (f32[8,32,512]{2,1,0:T(8,128)S(1)}, f32[8,32,512]{2,1,0:T(8,128)S(1)}, u32[]{:S(2)}, u32[]{:S(2)}) collective-permute-start(f32[8,32,512]{2,1,0:T(8,128)S(1)} %slice.98), channel_id=1, source_target_pairs={{0,2},{1,3},{2,0},{3,1},{4,6},{5,7},{6,4},{7,5},{8,10},{9,11},{10,... | collective-permute-start | bytes 1572872 | tf_op jit(solution)/shard_map/ppermute | solution.py:125
  9.5 0.4 %collective-permute-start.1 = (f32[1]{0:T(128)}, f32[1]{0:T(128)}, u32[]{:S(2)}, u32[]{:S(2)}) collective-permute-start(f32[1]{0:T(128)} %param.11), channel_id=1, source_target_pairs={{0,16},{16,0},{1,17},{17,1},{2,18},{18,2},{3,19},{19,3},{4,20},{20... | collective-permute-start | bytes 20 | tf_op jit(solution)/shard_map/ppermute | solution.py:138
  11.3 0.0 collective-permute-done.1
  11.9 3.1 %collective-permute-done = f32[8,32,512]{2,1,0:T(8,128)S(1)} collective-permute-done((f32[8,32,512]{2,1,0:T(8,128)S(1)}, f32[8,32,512]{2,1,0:T(8,128)S(1)}, u32[]{:S(2)}, u32[]{:S(2)}) %collective-permute-start) | collective-permute-done | bytes 524320 | tf_op jit(solution)/shard_map/ppermute | solution.py:125
  15.0 0.1 slice_add_fusion.3
  15.1 2.1 %collective-permute-start.2 = (f32[4,32,512]{2,1,0:T(8,128)S(1)}, f32[4,32,512]{2,1,0:T(8,128)S(1)}, u32[]{:S(2)}, u32[]{:S(2)}) collective-permute-start(f32[4,32,512]{2,1,0:T(8,128)S(1)} %get-tuple-element.20), channel_id=1, source_target_pairs={{0,2},{1,3},{2,0},{3,1},{4,6},{5,7},{6,4},{7,5},{8,10},{9,11},{10,... | collective-permute-start | bytes 786440 | tf_op jit(solution)/shard_map/ppermute | solution.py:125
  17.2 0.0 collective-permute-done.5
  17.2 0.1 slice_add_fusion.1
  17.3 1.6 %collective-permute-start.6 = (f32[4,32,512]{2,1,0:T(8,128)S(1)}, f32[4,32,512]{2,1,0:T(8,128)S(1)}, u32[]{:S(2)}, u32[]{:S(2)}) collective-permute-start(f32[4,32,512]{2,1,0:T(8,128)S(1)} %get-tuple-element.22), channel_id=1, source_target_pairs={{0,4},{1,5},{2,6},{3,7},{4,0},{5,1},{6,2},{7,3},{8,12},{9,13},{10,... | collective-permute-start | bytes 786440 | tf_op jit(solution)/shard_map/ppermute | solution.py:125
  19.0 2.6 %collective-permute-done.2 = f32[4,32,512]{2,1,0:T(8,128)S(1)} collective-permute-done((f32[4,32,512]{2,1,0:T(8,128)S(1)}, f32[4,32,512]{2,1,0:T(8,128)S(1)}, u32[]{:S(2)}, u32[]{:S(2)}) %collective-permute-start.2) | collective-permute-done | bytes 262176 | tf_op jit(solution)/shard_map/ppermute | solution.py:125
  21.6 2.1 %collective-permute-start.3 = (f32[2,32,512]{2,1,0:T(8,128)S(1)}, f32[2,32,512]{2,1,0:T(8,128)S(1)}, u32[]{:S(2)}, u32[]{:S(2)}) collective-permute-start(f32[2,32,512]{2,1,0:T(8,128)S(1)} %get-tuple-element.24), channel_id=1, source_target_pairs={{0,4},{1,5},{2,6},{3,7},{4,0},{5,1},{6,2},{7,3},{8,12},{9,13},{10,... | collective-permute-start | bytes 393224 | tf_op jit(solution)/shard_map/ppermute | solution.py:125
  23.8 0.4 collective-permute-done.6
  24.2 2.3 %collective-permute-start.7 = (f32[2,32,512]{2,1,0:T(8,128)S(1)}, f32[2,32,512]{2,1,0:T(8,128)S(1)}, u32[]{:S(2)}, u32[]{:S(2)}) collective-permute-start(f32[2,32,512]{2,1,0:T(8,128)S(1)} %get-tuple-element.26), channel_id=1, source_target_pairs={{0,8},{1,9},{2,10},{3,11},{4,12},{5,13},{6,14},{7,15},{8,0},{9,1},... | collective-permute-start | bytes 393224 | tf_op jit(solution)/shard_map/ppermute | solution.py:125
  26.5 0.3 collective-permute-done.3
  26.7 4.3 %collective-permute-start.4 = (f32[1,32,512]{2,1,0:T(8,128)S(1)}, f32[1,32,512]{2,1,0:T(8,128)S(1)}, u32[]{:S(2)}, u32[]{:S(2)}) collective-permute-start(f32[1,32,512]{2,1,0:T(8,128)S(1)} %slice_add_fusion.10), channel_id=1, source_target_pairs={{0,8},{1,9},{2,10},{3,11},{4,12},{5,13},{6,14},{7,15},{8,0},{9,1},... | collective-permute-start | bytes 196616 | tf_op jit(solution)/shard_map/ppermute | solution.py:125
  31.1 0.0 collective-permute-done.7
  31.1 1.5 %collective-permute-start.8 = (f32[1,32,512]{2,1,0:T(8,128)S(1)}, f32[1,32,512]{2,1,0:T(8,128)S(1)}, u32[]{:S(2)}, u32[]{:S(2)}) collective-permute-start(f32[1,32,512]{2,1,0:T(8,128)S(1)} %slice_add_fusion.8), channel_id=1, source_target_pairs={{0,1},{1,0},{2,3},{3,2},{4,5},{5,4},{6,7},{7,6},{8,9},{9,8},{10,11... | collective-permute-start | bytes 196616 | tf_op jit(solution)/shard_map/ppermute | solution.py:125
  32.6 1.5 %collective-permute-done.4 = f32[1,32,512]{2,1,0:T(8,128)S(1)} collective-permute-done((f32[1,32,512]{2,1,0:T(8,128)S(1)}, f32[1,32,512]{2,1,0:T(8,128)S(1)}, u32[]{:S(2)}, u32[]{:S(2)}) %collective-permute-start.4) | collective-permute-done | bytes 65568 | tf_op jit(solution)/shard_map/ppermute | solution.py:125
  34.1 1.3 %collective-permute-done.8 = f32[1,32,512]{2,1,0:T(8,128)S(1)} collective-permute-done((f32[1,32,512]{2,1,0:T(8,128)S(1)}, f32[1,32,512]{2,1,0:T(8,128)S(1)}, u32[]{:S(2)}, u32[]{:S(2)}) %collective-permute-start.8) | collective-permute-done | bytes 65568 | tf_op jit(solution)/shard_map/ppermute | solution.py:125
  35.4 0.0 copy-done
  35.4 0.0 copy-done.1
  35.4 0.0 copy-done.2
  35.4 0.8 %multiply_subtract_fusion = (f32[1,64,512]{2,1,0:T(8,128)S(1)}, f32[1,64,512]{2,1,0:T(8,128)}, f32[1,64,512]{2,1,0:T(8,128)}) fusion(f32[1,64,512]{2,1,0:T(8,128)S(1)} %copy-done, f32[]{:T(128)} %bitcast.5, f32[]{:T(128)} %bitcast.2, f32[]{:T(128)} %bitcast.1, f32[]{:T(128)} %bitcast, f32[]{:T(128)} %bitcast.3, f32[1,32,512]{2,1,0:T(8,128)S(1)} %fusion.1, ...), kind=kLoop, calls=%fused_computation.12 | loop fusion | flops 589824 | bytes 917524 | tf_op jit(solution)/shard_map/sub | solution.py:178
  36.3 0.6 %collective-permute-start.9 = (f32[1,64,512]{2,1,0:T(8,128)S(1)}, f32[1,64,512]{2,1,0:T(8,128)S(1)}, u32[]{:S(2)}, u32[]{:S(2)}) collective-permute-start(f32[1,64,512]{2,1,0:T(8,128)S(1)} %get-tuple-element.16), channel_id=1, source_target_pairs={{0,16},{16,0},{1,17},{17,1},{2,18},{18,2},{3,19},{19,3},{4,20},{20... | collective-permute-start | bytes 393224 | tf_op jit(solution)/shard_map/ppermute | solution.py:138
  36.8 1.0 %collective-permute-done.9 = f32[1,64,512]{2,1,0:T(8,128)S(1)} collective-permute-done((f32[1,64,512]{2,1,0:T(8,128)S(1)}, f32[1,64,512]{2,1,0:T(8,128)S(1)}, u32[]{:S(2)}, u32[]{:S(2)}) %collective-permute-start.9) | collective-permute-done | bytes 131104 | tf_op jit(solution)/shard_map/ppermute | solution.py:138
  37.8 0.7 %multiply_add_fusion = f32[1,64,512]{2,1,0:T(8,128)} fusion(f32[1,64,512]{2,1,0:T(8,128)S(1)} %collective-permute-done.9, f32[1,64,512]{2,1,0:T(8,128)S(1)} %get-tuple-element.16), kind=kLoop, calls=%fused_computation.11 | loop fusion | flops 98304 | bytes 393216 | tf_op jit(solution)/shard_map/add | solution.py:181
  (8 shorter events, 0.2 us)
Async XLA Ops:
  4.9 10.2 %collective-permute-start = (f32[8,32,512]{2,1,0:T(8,128)S(1)}, f32[8,32,512]{2,1,0:T(8,128)S(1)}, u32[]{:S(2)}, u32[]{:S(2)}) collective-permute-start(f32[8,32,512]{2,1,0:T(8,128)S(1)} %slice.85), channel_id=1, source_target_pairs={{0,1},{1,0},{2,3},{3,2},{4,5},{5,4},{6,7},{7,6},{8,9},{9,8},{10,11... | collective-permute-start | bytes 1572872 | tf_op jit(solution)/shard_map/ppermute | solution.py:125
  7.9 27.5 %copy-start = (f32[1,64,512]{2,1,0:T(8,128)S(1)}, f32[1,64,512]{2,1,0:T(8,128)}, u32[]{:S(2)}) copy-start(f32[1,64,512]{2,1,0:T(8,128)} %param.10) | copy-start | bytes 393220
  7.9 27.6 %copy-start.1 = (f32[1,64,512]{2,1,0:T(8,128)S(1)}, f32[1,64,512]{2,1,0:T(8,128)}, u32[]{:S(2)}) copy-start(f32[1,64,512]{2,1,0:T(8,128)} %param.13) | copy-start | bytes 393220
  7.9 27.6 %copy-start.2 = (f32[1,64,512]{2,1,0:T(8,128)S(1)}, f32[1,64,512]{2,1,0:T(8,128)}, u32[]{:S(2)}) copy-start(f32[1,64,512]{2,1,0:T(8,128)} %param.12) | copy-start | bytes 393220
  7.9 9.3 %collective-permute-start.5 = (f32[8,32,512]{2,1,0:T(8,128)S(1)}, f32[8,32,512]{2,1,0:T(8,128)S(1)}, u32[]{:S(2)}, u32[]{:S(2)}) collective-permute-start(f32[8,32,512]{2,1,0:T(8,128)S(1)} %slice.98), channel_id=1, source_target_pairs={{0,2},{1,3},{2,0},{3,1},{4,6},{5,7},{6,4},{7,5},{8,10},{9,11},{10,... | collective-permute-start | bytes 1572872 | tf_op jit(solution)/shard_map/ppermute | solution.py:125
  9.5 1.8 %collective-permute-start.1 = (f32[1]{0:T(128)}, f32[1]{0:T(128)}, u32[]{:S(2)}, u32[]{:S(2)}) collective-permute-start(f32[1]{0:T(128)} %param.11), channel_id=1, source_target_pairs={{0,16},{16,0},{1,17},{17,1},{2,18},{18,2},{3,19},{19,3},{4,20},{20... | collective-permute-start | bytes 20 | tf_op jit(solution)/shard_map/ppermute | solution.py:138
  15.1 6.5 %collective-permute-start.2 = (f32[4,32,512]{2,1,0:T(8,128)S(1)}, f32[4,32,512]{2,1,0:T(8,128)S(1)}, u32[]{:S(2)}, u32[]{:S(2)}) collective-permute-start(f32[4,32,512]{2,1,0:T(8,128)S(1)} %get-tuple-element.20), channel_id=1, source_target_pairs={{0,2},{1,3},{2,0},{3,1},{4,6},{5,7},{6,4},{7,5},{8,10},{9,11},{10,... | collective-permute-start | bytes 786440 | tf_op jit(solution)/shard_map/ppermute | solution.py:125
  17.3 6.8 %collective-permute-start.6 = (f32[4,32,512]{2,1,0:T(8,128)S(1)}, f32[4,32,512]{2,1,0:T(8,128)S(1)}, u32[]{:S(2)}, u32[]{:S(2)}) collective-permute-start(f32[4,32,512]{2,1,0:T(8,128)S(1)} %get-tuple-element.22), channel_id=1, source_target_pairs={{0,4},{1,5},{2,6},{3,7},{4,0},{5,1},{6,2},{7,3},{8,12},{9,13},{10,... | collective-permute-start | bytes 786440 | tf_op jit(solution)/shard_map/ppermute | solution.py:125
  21.6 5.1 %collective-permute-start.3 = (f32[2,32,512]{2,1,0:T(8,128)S(1)}, f32[2,32,512]{2,1,0:T(8,128)S(1)}, u32[]{:S(2)}, u32[]{:S(2)}) collective-permute-start(f32[2,32,512]{2,1,0:T(8,128)S(1)} %get-tuple-element.24), channel_id=1, source_target_pairs={{0,4},{1,5},{2,6},{3,7},{4,0},{5,1},{6,2},{7,3},{8,12},{9,13},{10,... | collective-permute-start | bytes 393224 | tf_op jit(solution)/shard_map/ppermute | solution.py:125
  24.2 6.9 %collective-permute-start.7 = (f32[2,32,512]{2,1,0:T(8,128)S(1)}, f32[2,32,512]{2,1,0:T(8,128)S(1)}, u32[]{:S(2)}, u32[]{:S(2)}) collective-permute-start(f32[2,32,512]{2,1,0:T(8,128)S(1)} %get-tuple-element.26), channel_id=1, source_target_pairs={{0,8},{1,9},{2,10},{3,11},{4,12},{5,13},{6,14},{7,15},{8,0},{9,1},... | collective-permute-start | bytes 393224 | tf_op jit(solution)/shard_map/ppermute | solution.py:125
  26.7 7.4 %collective-permute-start.4 = (f32[1,32,512]{2,1,0:T(8,128)S(1)}, f32[1,32,512]{2,1,0:T(8,128)S(1)}, u32[]{:S(2)}, u32[]{:S(2)}) collective-permute-start(f32[1,32,512]{2,1,0:T(8,128)S(1)} %slice_add_fusion.10), channel_id=1, source_target_pairs={{0,8},{1,9},{2,10},{3,11},{4,12},{5,13},{6,14},{7,15},{8,0},{9,1},... | collective-permute-start | bytes 196616 | tf_op jit(solution)/shard_map/ppermute | solution.py:125
  31.1 4.3 %collective-permute-start.8 = (f32[1,32,512]{2,1,0:T(8,128)S(1)}, f32[1,32,512]{2,1,0:T(8,128)S(1)}, u32[]{:S(2)}, u32[]{:S(2)}) collective-permute-start(f32[1,32,512]{2,1,0:T(8,128)S(1)} %slice_add_fusion.8), channel_id=1, source_target_pairs={{0,1},{1,0},{2,3},{3,2},{4,5},{5,4},{6,7},{7,6},{8,9},{9,8},{10,11... | collective-permute-start | bytes 196616 | tf_op jit(solution)/shard_map/ppermute | solution.py:125
  36.3 1.6 %collective-permute-start.9 = (f32[1,64,512]{2,1,0:T(8,128)S(1)}, f32[1,64,512]{2,1,0:T(8,128)S(1)}, u32[]{:S(2)}, u32[]{:S(2)}) collective-permute-start(f32[1,64,512]{2,1,0:T(8,128)S(1)} %get-tuple-element.16), channel_id=1, source_target_pairs={{0,16},{16,0},{1,17},{17,1},{2,18},{18,2},{3,19},{19,3},{4,20},{20... | collective-permute-start | bytes 393224 | tf_op jit(solution)/shard_map/ppermute | solution.py:138
